TPU v7x, 512 devices: a whole 4x8x8 slice. The times are simulated.
512 devices in a mesh: dom: 256 (over z, y, x), blk: 2 (over core).
Axes of the slice: x: 4, y: 8, z: 8, core: 2. Of those that a mesh axis runs over, the one named last changes fastest.
Arguments:
- pd_disp: float32 [1024, 2, 128], P(('dom', 'blk')), may hold values from -4 to 4
- pd_vel: float32 [1024, 2, 128], P(('dom', 'blk')), may hold values from -4 to 4
- pd_coord: float32 [1024, 2, 128], P(('dom', 'blk')), may hold values from -4 to 4
- pd_modulus: float32 [1024, 128], P(('dom', 'blk')), may hold values from 2 to 20
- pd_step: float32 [1024, 128], P(('dom', 'blk')), may hold values from 0.03 to 0.3
- family_tile_lists: int32 [1024, 3], P(('dom', 'blk')), may hold values from 0 to 11, as said below
- live_tiles: int32 [256], P('dom'), may hold values from 3 to 4, as said below
- patch_tile: int32 [512], P('dom'), may hold values from 0 to 3, as said below
- patch_blend: float32 [512, 128], P('dom'), may hold values from 0.1 to 0.9
- patch_nodes: int32 [512, 128], P(('dom', 'blk')), may hold values from 0 to 12799, as said below
- patch_matrix: float32 [512, 128, 128], P(('dom', 'blk')), may hold values from -0.5 to 0.5
- fe_disp: float32 [2, 3276800], P(None, ('dom', 'blk')), may hold values from -4 to 4
- fe_vel: float32 [2, 3276800], P(None, ('dom', 'blk')), may hold values from -4 to 4
- fe_step: float32 [3276800], P(('dom', 'blk')), may hold values from 0.03 to 0.3
- fe_modulus: float32 [65536], P(('dom', 'blk')), may hold values from 0.5 to 2
- element_nodes: int32 [64, 65536], P(None, ('dom', 'blk')), may hold values from 0 to 12799, as said below
- shape_grad: float32 [2, 64, 64], replicated, may hold values from -0.75 to 0.75
- quad_weight: float32 [64], replicated, may hold values from 0.5 to 2
- shared_left: int32 [256, 113], P('dom'), may hold values from 0 to 12799, as said below
- shared_right: int32 [256, 113], P('dom'), may hold values from 0 to 12799, as said below
Outputs:
- pd_disp_out: float32 [1024, 2, 128], P(('dom', 'blk'))
- pd_vel_out: float32 [1024, 2, 128], P(('dom', 'blk'))
- fe_disp_out: float32 [2, 3276800], P(None, ('dom', 'blk'))
- fe_vel_out: float32 [2, 3276800], P(None, ('dom', 'blk'))
Inputs may be any that keep to these rules, and one draw needn't show every extreme that they name: Local tiles at index live_tiles[d] or above in subdomain d are padding: their inputs are ignored and their outputs are zero. `family_tile_lists`: each entry names a live tile by extended index; the first subdomain names no entry below 4, the last none at 8 or above. `patch_tile`: within a subdomain the 2 patch tiles are distinct live tiles. `patch_nodes`: node ids of a subdomain's patches are distinct and belong to its elements. `element_nodes`: local node ids of each element's subdomain. `shared_left`: row d lists distinct nodes; entry r is the same physical node as shared_right[d - 1, r]. `shared_right`: row d lists distinct nodes, none in shared_left[d].
All inputs are finite; a program needn't handle non-finite values.
Results may differ from a plain program's by a relative error of at most 0.0003.
Values sent between devices are 32-bit elements; how exact they have to be, the bound alone decides.
A program may use at most 64 MiB of HBM per device.

v0:
```python
import jax
import jax.numpy as jnp
from jax import lax
from jax.sharding import PartitionSpec as P

time_step = 0.5
horizon_sq = 2.0
core_sq = 0.01
stretch_scale = 0.3


def with_halo(cells, sides, width):
    for axis, dim in sides:
        count = lax.axis_size(axis)
        ends = count - 1
        head = lax.slice_in_dim(cells, 0, width, axis=dim)
        tail = lax.slice_in_dim(cells, cells.shape[dim] - width, cells.shape[dim], axis=dim)
        cells = jnp.concatenate(
            [
                lax.ppermute(tail, axis, [(i, (i + 1) % count) for i in range(ends)]),
                cells,
                lax.ppermute(head, axis, [((i + 1) % count, i) for i in range(ends)]),
            ],
            axis=dim,
        )
    return cells


def bond_terms(x_own, u_own, x_far, u_far):
    offset = x_far[:, :, None, :] - x_own[None, :, :, None]
    deformed = offset + u_far[:, :, None, :] - u_own[None, :, :, None]
    rest_sq = jnp.sum(offset * offset, axis=1)
    rest_len = jnp.sqrt(rest_sq + core_sq)
    length = jnp.sqrt(jnp.sum(deformed * deformed, axis=1) + core_sq)
    stretch = length - rest_len
    ratio = stretch / stretch_scale
    influence = jnp.exp(-rest_sq / horizon_sq) / (1.0 + ratio * ratio)
    return (deformed, length, rest_len, stretch, influence)


def dilatation(x_own, u_own, x_far, u_far):
    deformed, length, rest_len, stretch, influence = bond_terms(x_own, u_own, x_far, u_far)
    point_volume = jnp.sum(influence * rest_len * rest_len, axis=(0, 2))
    volumetric_dilatation = (
        2.0 * jnp.sum(influence * rest_len * stretch, axis=(0, 2)) / point_volume
    )
    return (volumetric_dilatation, point_volume)


def bond_force(x_own, u_own, x_far, u_far, k_own, th_own, m_own, k_far, th_far, m_far):
    deformed, length, rest_len, stretch, influence = bond_terms(x_own, u_own, x_far, u_far)
    ko, to, mo = (k_own[None, :, None], th_own[None, :, None], m_own[None, :, None])
    kf, tf, mf = (k_far[:, None, :], th_far[:, None, :], m_far[:, None, :])
    t_own = influence * (
        2.0 * ko * to * rest_len / mo + 4.0 * ko * (stretch - 0.5 * to * rest_len) / mo
    )
    t_far = influence * (
        2.0 * kf * tf * rest_len / mf + 4.0 * kf * (stretch - 0.5 * tf * rest_len) / mf
    )
    scalar = (t_own + t_far) / length
    return jnp.sum(scalar[:, None] * deformed, axis=(0, 3))


def element_force(disp_el, modulus, shape_grad, quad_weight):
    precise = lax.Precision.HIGHEST
    grad = jnp.einsum("aqn,cne->caqe", shape_grad, disp_el, precision=precise)
    strain_xx = grad[0, 0]
    strain_yy = grad[1, 1]
    strain_xy = 0.5 * (grad[0, 1] + grad[1, 0])
    stiffen = 1.0 + strain_xx * strain_xx + strain_yy * strain_yy + 2.0 * strain_xy * strain_xy
    scaled = modulus[None, :] * quad_weight[:, None] * stiffen
    trace_sum = strain_xx + strain_yy
    s_xx = scaled * (trace_sum + 2.0 * strain_xx)
    s_yy = scaled * (trace_sum + 2.0 * strain_yy)
    s_xy = scaled * 2.0 * strain_xy
    stress = jnp.stack([jnp.stack([s_xx, s_xy]), jnp.stack([s_xy, s_yy])])
    return jnp.einsum("aqn,caqe->cne", shape_grad, stress, precision=precise)


def select_rows(wanted, first, count):
    slots = first + jnp.arange(count, dtype=jnp.int32)
    return (wanted[:, None] == slots[None, :]).astype(jnp.float32)


def blend_tiles(table, first, targets, patch_tile, patch_blend):
    precise = lax.Precision.HIGHEST
    choose = select_rows(patch_tile, first, table.shape[0])
    current = jnp.einsum("pk,kcn->pcn", choose, table, precision=precise)
    delta = patch_blend[:, None, :] * (targets - current)
    return table + jnp.einsum("pk,pcn->kcn", choose, delta, precision=precise)


def shards(
    pd_disp,
    pd_vel,
    pd_coord,
    pd_modulus,
    pd_step,
    family_tile_lists,
    live_tiles,
    patch_tile,
    patch_blend,
    patch_nodes,
    patch_matrix,
    fe_disp,
    fe_vel,
    fe_step,
    fe_modulus,
    element_nodes,
    shape_grad,
    quad_weight,
    shared_left,
    shared_right,
):
    precise = lax.Precision.HIGHEST
    blocks = lax.axis_size("blk")
    rank = lax.axis_index("blk")
    tiles_dev = pd_disp.shape[0]
    tiles_dom = tiles_dev * blocks
    patches_dev = patch_matrix.shape[0]
    active_flags = live_tiles[0]
    counter = jnp.arange(tiles_dev, dtype=jnp.int32)
    static_own = jnp.concatenate([pd_coord, pd_modulus[:, None, :]], axis=1)
    static_dom = lax.all_gather(static_own, "blk", axis=0, tiled=True)
    static_ext = with_halo(static_dom, (("dom", 0),), tiles_dom)
    coord_ext = static_ext[:, :2]
    modulus_ext = static_ext[:, 2]
    sorting_permutation = rank * tiles_dev + counter
    my_tiles = lax.dynamic_slice_in_dim(patch_tile, rank * patches_dev, patches_dev)
    my_blend = lax.dynamic_slice_in_dim(patch_blend, rank * patches_dev, patches_dev)
    alive = (rank * tiles_dev + counter < active_flags).astype(jnp.float32)[:, None, None]
    left_ids = shared_left[0]
    right_ids = shared_right[0]
    for section in range(2):
        fe_table = lax.all_gather(fe_disp, "blk", axis=1, tiled=True)
        picked = fe_table[:, patch_nodes]
        target = jnp.einsum("qpn,cqn->qcp", patch_matrix, picked, precision=precise)
        targets = lax.all_gather(target, "blk", axis=0, tiled=True)
        table = lax.all_gather(pd_disp, "blk", axis=0, tiled=True)
        blended = blend_tiles(table, 0, targets, patch_tile, patch_blend)
        disp_ext = with_halo(blended, (("dom", 0),), tiles_dom)
        own_blended = lax.dynamic_slice_in_dim(blended, rank * tiles_dev, tiles_dev)

        def dilatation_single_tile(packed_rows):
            tile_number, rows = packed_rows
            own = tiles_dom + tile_number

            def dilatation_run(discarded_output):
                volumetric_dilatation, point_volume = dilatation(
                    coord_ext[own], disp_ext[own], coord_ext[rows], disp_ext[rows]
                )
                return jnp.stack([volumetric_dilatation, point_volume])

            def dilatation_skip(discarded_output):
                return jnp.stack([jnp.zeros_like(modulus_ext[0]), jnp.ones_like(modulus_ext[0])])

            return lax.cond(tile_number < active_flags, dilatation_run, dilatation_skip, None)

        bond_state = lax.map(dilatation_single_tile, (sorting_permutation, family_tile_lists))
        state_dom = lax.all_gather(bond_state, "blk", axis=0, tiled=True)
        state_ext = with_halo(state_dom, (("dom", 0),), tiles_dom)

        def force_one(packed_rows):
            tile_number, rows = packed_rows
            own = tiles_dom + tile_number

            def force_run(discarded_output):
                return bond_force(
                    coord_ext[own],
                    disp_ext[own],
                    coord_ext[rows],
                    disp_ext[rows],
                    modulus_ext[own],
                    state_ext[own, 0],
                    state_ext[own, 1],
                    modulus_ext[rows],
                    state_ext[rows, 0],
                    state_ext[rows, 1],
                )

            def force_skip(discarded_output):
                return jnp.zeros_like(coord_ext[0])

            return lax.cond(tile_number < active_flags, force_run, force_skip, None)

        forces = lax.map(force_one, (sorting_permutation, family_tile_lists))
        forces_dom = lax.all_gather(forces, "blk", axis=0, tiled=True)
        own_force = lax.dynamic_slice_in_dim(forces_dom, rank * tiles_dev, tiles_dev)
        pd_vel = (pd_vel + pd_step[:, None, :] * own_force) * alive
        pd_disp = (own_blended + time_step * pd_vel) * alive
        choose = select_rows(my_tiles, 0, tiles_dom)
        patch_force = jnp.einsum("qk,kcn->qcn", choose, forces_dom, precision=precise)
        weighted = patch_force * my_blend[:, None, :]
        reaction = jnp.einsum("qpn,qcp->cqn", patch_matrix, weighted, precision=precise)
        disp_el = fe_table[:, element_nodes]
        forces_el = element_force(disp_el, fe_modulus, shape_grad, quad_weight)
        nodal = (
            jnp.zeros(fe_table.shape, jnp.float32)
            .at[:, element_nodes.reshape(-1)]
            .add(forces_el.reshape(2, -1))
        )
        nodal = -nodal
        nodal = nodal.at[:, patch_nodes.reshape(-1)].add(reaction.reshape(2, -1))
        sides = jnp.stack([nodal[:, left_ids], nodal[:, right_ids]])
        border = with_halo(sides, (("dom", 0),), 1)
        nodal = nodal.at[:, left_ids].add(border[0]).at[:, right_ids].add(border[3])
        total = lax.psum_scatter(nodal, "blk", scatter_dimension=1, tiled=True)
        fe_vel = fe_vel + fe_step[None, :] * total
        fe_disp = fe_disp + time_step * fe_vel
    return (pd_disp, pd_vel, fe_disp, fe_vel)


def solution(mesh):
    return jax.shard_map(
        shards,
        mesh=mesh,
        in_specs=(
            P(("dom", "blk"), None, None),
            P(("dom", "blk"), None, None),
            P(("dom", "blk"), None, None),
            P(("dom", "blk"), None),
            P(("dom", "blk"), None),
            P(("dom", "blk"), None),
            P("dom"),
            P("dom"),
            P("dom", None),
            P(("dom", "blk"), None),
            P(("dom", "blk"), None, None),
            P(None, ("dom", "blk")),
            P(None, ("dom", "blk")),
            P(("dom", "blk")),
            P(("dom", "blk")),
            P(None, ("dom", "blk")),
            P(),
            P(),
            P("dom", None),
            P("dom", None),
        ),
        out_specs=(
            P(("dom", "blk"), None, None),
            P(("dom", "blk"), None, None),
            P(None, ("dom", "blk")),
            P(None, ("dom", "blk")),
        ),
        check_vma=False,
    )
```

profile of v0, /device:TPU:1, one launch (start us, length us, event | category | flops | bytes accessed | tf_op | source)
XLA Modules:
  0.0 450.9 jit_solution(7940313090664460190)
XLA Ops:
  7.9 8.4 %all_gather.36 = f32[4,3,128]{2,1,0:T(4,128)S(1)} all-gather(f32[2,3,128]{2,1,0:T(4,128)S(1)} %pad_maximum_fusion.4), channel_id=1, replica_groups=mesh['dom'=256,'blk'=2] {'blk'}, dimensions={0}, use_global_device_ids=true | all-gather | bytes 9216 | tf_op jit(solution)/shard_map/all_gather | solution.py:124
  22.8 6.8 %all_gather.34 = f32[2,12800]{0,1:T(8,128)} all-gather(f32[2,6400]{0,1:T(8,128)S(1)} %copy.148), channel_id=1, replica_groups=mesh['dom'=256,'blk'=2] {'blk'}, dimensions={1}, use_global_device_ids=true | all-gather | bytes 153600 | tf_op jit(solution)/shard_map/all_gather | solution.py:135
  36.8 4.9 %collective-permute-start.2 = (f32[4,2,128]{2,0,1:T(4,128)S(1)}, f32[4,2,128]{2,0,1:T(4,128)S(1)}, u32[]{:S(2)}, u32[]{:S(2)}) collective-permute-start(f32[4,2,128]{2,0,1:T(4,128)S(1)} %convolution_add_fusion.1), channel_id=1, source_target_pairs={{0,2},{2,4},{4,6},{6,8},{8,10},{10,12},{12,14},{14,16},{16,18},{18... | collective-permute-start | bytes 12296 | tf_op jit(solution)/shard_map/ppermute | solution.py:20
  41.8 30.6 %gather_fusion.15 = f32[8192,2]{1,0:T(8,128)} fusion(f32[2,12800]{0,1:T(8,128)} %all_gather.34, s32[8192]{0:T(1024)S(1)} %fusion.75), kind=kCustom, calls=%fused_computation.15 | custom fusion | bytes 163840 | tf_op jit(solution)/shard_map/gather | solution.py:195
  76.2 9.8 %while.40 = (s32[]{:T(128)}, f32[2,2,128]{2,1,0:T(2,128)S(1)}, s32[2]{0:T(128)S(1)}, s32[]{:T(128)}, s32[2,3]{1,0:T(2,128)S(1)}, /*index=5*/f32[12,2,128]{2,1,0:T(2,128)S(1)}, f32[12,2,128]{2,1,0:T(2,128)S(1)}, s32[]{:T(128)}) while((s32[]{:T(128)}, f32[2,2,128]{2,1,0:T(2,128)S(1)}, s32[2]{0:T(128)S(1)}, s32[]{:T(128)}, s32[2,3]{1,0:T(2,128)S(1)}, ...), condition=%wide.region_7.8_spmd, body=%wide.region_0.7_spmd.sunk | while | flops 1279249 | bytes 822045 | solution.py:159
  97.4 47.4 %scatter_custom_fusion = f32[2,12800]{0,1:T(8,128)} fusion(s32[8192]{0:T(1024)S(1)} %bitcast.304, f32[8192,2]{1,0:T(8,128)} %bitcast.295, f32[]{:T(128)} %constant.284.clone.1), kind=kCustom, calls=%fused_computation.146 | custom fusion | flops 16384 | bytes 102912 | tf_op jit(solution)/shard_map/scatter-add | solution.py:200
  144.8 4.9 %neg.34 = f32[2,12800]{0,1:T(8,128)} negate(f32[2,12800]{0,1:T(8,128)} %scatter_custom_fusion) | non-fusion elementwise | flops 25600 | bytes 204800 | tf_op jit(solution)/shard_map/neg | solution.py:202
  149.8 14.0 %while.41 = (s32[]{:T(128)}, f32[2,2,128]{2,1,0:T(2,128)S(1)}, s32[2]{0:T(128)S(1)}, s32[]{:T(128)}, s32[2,3]{1,0:T(2,128)S(1)}, /*index=5*/f32[12,2,128]{2,1,0:...) while((s32[]{:T(128)}, f32[2,2,128]{2,1,0:T(2,128)S(1)}, ...), condition=%wide.region_14.15_spmd, body=%wide.region_8.14_spmd.sunk | while | flops 2362144 | bytes 1249193 | solution.py:186
  151.7 5.1 %conditional.9 = (f32[1,2,128]{2,1,0:T(2,128)S(1)}) conditional(s32[]{:T(128)} %convert_element_type.30, () %tuple.177, (s32[2,3]{1,0:T(2,128)S(1)}, s32[]{:T(128)}, f32[12,2,128]{2,1,0:T(2,128)S(1)}, s32[]{:T(128)}, f32[12,2,128]{2,1,0:T(2,128)S(1)}, /*index=5*/f32[12,128]{1,0:T(8,128)S(1)}, f32[12,2,128]{2,1,0:T(2,128)S(1)}) %tuple.178), branch_computations={%region_9.9_spmd, %region_10.13_spmd} | conditional | flops 2362140 | bytes 1246950 | solution.py:184
  158.7 5.1 %conditional.9 = (f32[1,2,128]{2,1,0:T(2,128)S(1)}) conditional(s32[]{:T(128)} %convert_element_type.30, () %tuple.177, (s32[2,3]{1,0:T(2,128)S(1)}, s32[]{:T(128)}, f32[12,2,128]{2,1,0:T(2,128)S(1)}, s32[]{:T(128)}, f32[12,2,128]{2,1,0:T(2,128)S(1)}, /*index=5*/f32[12,128]{1,0:T(8,128)S(1)}, f32[12,2,128]{2,1,0:T(2,128)S(1)}) %tuple.178), branch_computations={%region_9.9_spmd, %region_10.13_spmd} | conditional | flops 2362140 | bytes 1246950 | solution.py:184
  166.9 6.7 %scatter_fusion = f32[2,12800]{0,1:T(8,128)} fusion(f32[2,12800]{0,1:T(8,128)} %neg.34, s32[128]{0:T(128)S(1)} %fusion.97, f32[128,2]{1,0:T(8,128)S(1)} %copy.160), kind=kCustom, calls=%fused_computation.23 | custom fusion | flops 256 | bytes 3584 | tf_op jit(solution)/shard_map/scatter-add | solution.py:203
  185.6 6.7 %scatter_custom_fusion.2 = f32[2,12800]{0,1:T(8,128)} fusion(f32[2,12800]{0,1:T(8,128)} %scatter_fusion, s32[113]{0:T(128)S(1)} %fusion.98, f32[1,2,113]{1,2,0:T(8,128)S(1)} %collective-permute-done.6), kind=kCustom, calls=%fused_computation.190 | custom fusion | flops 226 | bytes 163840 | tf_op jit(solution)/shard_map/scatter-add | solution.py:206
  192.3 6.7 %scatter_custom_fusion.3 = f32[2,12800]{0,1:T(8,128)} fusion(f32[2,12800]{0,1:T(8,128)} %scatter_custom_fusion.2, s32[113]{0:T(128)S(1)} %fusion.99, f32[1,2,113]{1,2,0:T(8,128)S(1)} %collective-permute-done.7), kind=kCustom, calls=%fused_computation.188 | custom fusion | flops 226 | bytes 163840 | tf_op jit(solution)/shard_map/scatter-add | solution.py:206
  201.7 31.1 %reduce-scatter.7.cloned.1.call-done = f32[6400,2]{1,0:T(8,128)} async-done(((f32[12800,2]{1,0:T(8,128)}), f32[6400,2]{1,0:T(8,128)}) %reduce-scatter.7.cloned.1.call-update) | async-done | bytes 51216
  252.7 30.6 %gather_fusion.19 = f32[8192,2]{1,0:T(8,128)} fusion(f32[2,12800]{0,1:T(8,128)} %copy.162, s32[8192]{0:T(1024)S(1)} %fusion.75), kind=kCustom, calls=%fused_computation.19 | custom fusion | bytes 163840 | tf_op jit(solution)/shard_map/gather | solution.py:195
  286.6 9.7 %while.42 = (s32[]{:T(128)}, f32[2,2,128]{2,1,0:T(2,128)S(1)}, s32[2]{0:T(128)S(1)}, s32[]{:T(128)}, s32[2,3]{1,0:T(2,128)S(1)}, /*index=5*/f32[12,2,128]{2,1,0:T(2,128)S(1)}, f32[12,2,128]{2,1,0:T(2,128)S(1)}, s32[]{:T(128)}) while((s32[]{:T(128)}, f32[2,2,128]{2,1,0:T(2,128)S(1)}, s32[2]{0:T(128)S(1)}, s32[]{:T(128)}, ...), condition=%wide.region_27.28_spmd, body=%wide.region_20.27_spmd.sunk | while | flops 1279249 | bytes 822045 | solution.py:159
  307.0 47.4 %scatter_custom_fusion.4 = f32[2,12800]{0,1:T(8,128)} fusion(s32[8192]{0:T(1024)S(1)} %bitcast.305, f32[8192,2]{1,0:T(8,128)} %bitcast.294, f32[]{:T(128)} %constant.284.clone.1), kind=kCustom, calls=%fused_computation.144 | custom fusion | flops 16384 | bytes 102912 | tf_op jit(solution)/shard_map/scatter-add | solution.py:200
  359.3 14.0 %while.43 = (s32[]{:T(128)}, f32[2,2,128]{2,1,0:T(2,128)S(1)}, s32[2]{0:T(128)S(1)}, s32[]{:T(128)}, s32[2,3]{1,0:T(2,128)S(1)}, /*index=5*/f32[12,2,128]{2,1,0:...) while((s32[]{:T(128)}, f32[2,2,128]{2,1,0:T(2,128)S(1)}, ...), condition=%wide.region_34.35_spmd, body=%wide.region_28.34_spmd.sunk | while | flops 2362144 | bytes 1249193 | solution.py:186
  361.2 5.1 %conditional.11 = (f32[1,2,128]{2,1,0:T(2,128)S(1)}) conditional(s32[]{:T(128)} %convert_element_type.32, () %tuple.183, (s32[2,3]{1,0:T(2,128)S(1)}, s32[]{:T(128)}, f32[12,2,128]{2,1,0:T(2,128)S(1)}, s32[]{:T(128)}, f32[12,2,128]{2,1,0:T(2,128)S(1)}, /*index=5*/f32[12,128]{1,0:T(8,128)S(1)}, f32[12,2,128]{2,1,0:T(2,128)S(1)}) %tuple.184), branch_computations={%region_29.29_spmd, %region_30.33_spmd} | conditional | flops 2362140 | bytes 1246950 | solution.py:184
  368.2 5.1 %conditional.11 = (f32[1,2,128]{2,1,0:T(2,128)S(1)}) conditional(s32[]{:T(128)} %convert_element_type.32, () %tuple.183, (s32[2,3]{1,0:T(2,128)S(1)}, s32[]{:T(128)}, f32[12,2,128]{2,1,0:T(2,128)S(1)}, s32[]{:T(128)}, f32[12,2,128]{2,1,0:T(2,128)S(1)}, /*index=5*/f32[12,128]{1,0:T(8,128)S(1)}, f32[12,2,128]{2,1,0:T(2,128)S(1)}) %tuple.184), branch_computations={%region_29.29_spmd, %region_30.33_spmd} | conditional | flops 2362140 | bytes 1246950 | solution.py:184
  376.7 6.7 %scatter_fusion.1 = f32[2,12800]{0,1:T(8,128)} fusion(f32[2,12800]{0,1:T(8,128)} %neg.35, s32[128]{0:T(128)S(1)} %fusion.97, f32[128,2]{1,0:T(8,128)S(1)} %copy.173), kind=kCustom, calls=%fused_computation.27 | custom fusion | flops 256 | bytes 3584 | tf_op jit(solution)/shard_map/scatter-add | solution.py:203
  394.0 6.7 %scatter_custom_fusion.6 = f32[2,12800]{0,1:T(8,128)} fusion(f32[2,12800]{0,1:T(8,128)} %scatter_fusion.1, s32[113]{0:T(128)S(1)} %fusion.98, f32[1,2,113]{1,2,0:T(8,128)S(1)} %collective-permute-done.12), kind=kCustom, calls=%fused_computation.186 | custom fusion | flops 226 | bytes 163840 | tf_op jit(solution)/shard_map/scatter-add | solution.py:206
  400.6 6.7 %scatter_custom_fusion.7 = f32[2,12800]{0,1:T(8,128)} fusion(f32[2,12800]{0,1:T(8,128)} %scatter_custom_fusion.6, s32[113]{0:T(128)S(1)} %fusion.99, f32[1,2,113]{1,2,0:T(8,128)S(1)} %collective-permute-done.13), kind=kCustom, calls=%fused_computation.184 | custom fusion | flops 226 | bytes 163840 | tf_op jit(solution)/shard_map/scatter-add | solution.py:206
  408.6 32.3 %reduce-scatter.9.cloned.1.call-done = f32[6400,2]{1,0:T(8,128)} async-done(((f32[12800,2]{1,0:T(8,128)}), f32[6400,2]{1,0:T(8,128)}) %reduce-scatter.9.cloned.1.call-update) | async-done | bytes 51216
  (267 shorter events, 141.3 us)
Async XLA Ops:
  7.2 68.1 %copy-start = (f32[2,64,64]{2,1,0:T(8,128)S(1)}, f32[2,64,64]{2,1,0:T(8,128)}, u32[]{:S(2)}) copy-start(f32[2,64,64]{2,1,0:T(8,128)} %param.52) | copy-start | bytes 98308
  7.2 225.7 %reduce-scatter.7.cloned.1.call-start = ((), (), s32[]{:S(2)}) async-start(), calls=%async_computation.2 | async-start | bytes 9830400
  16.3 59.8 %collective-permute-start = (f32[4,3,128]{2,1,0:T(4,128)S(1)}, f32[4,3,128]{2,1,0:T(4,128)S(1)}, u32[]{:S(2)}, u32[]{:S(2)}) collective-permute-start(f32[4,3,128]{2,1,0:T(4,128)S(1)} %all_gather.36), channel_id=1, source_target_pairs={{0,2},{2,4},{4,6},{6,8},{8,10},{10,12},{12,14},{14,16},{16,18},{18... | collective-permute-start | bytes 18440 | tf_op jit(solution)/shard_map/ppermute | solution.py:20
  17.6 58.6 %collective-permute-start.1 = (f32[4,3,128]{2,1,0:T(4,128)S(1)}, f32[4,3,128]{2,1,0:T(4,128)S(1)}, u32[]{:S(2)}, u32[]{:S(2)}) collective-permute-start(f32[4,3,128]{2,1,0:T(4,128)S(1)} %all_gather.36), channel_id=1, source_target_pairs={{2,0},{4,2},{6,4},{8,6},{10,8},{12,10},{14,12},{16,14},{18,16},{20... | collective-permute-start | bytes 18440 | tf_op jit(solution)/shard_map/ppermute | solution.py:22
  22.7 52.8 %copy-start.9 = (f32[64]{0:T(128)S(1)}, f32[64]{0:T(128)}, u32[]{:S(2)}) copy-start(f32[64]{0:T(128)} %param.53) | copy-start | bytes 772
  22.7 52.8 %copy-start.10 = (f32[128]{0:T(128)S(1)}, f32[128]{0:T(128)}, u32[]{:S(2)}) copy-start(f32[128]{0:T(128)} %param.50) | copy-start | bytes 1540
  22.7 52.9 %copy-start.13 = (s32[1,113]{1,0:T(1,128)S(1)}, s32[1,113]{1,0:T(1,128)}, u32[]{:S(2)}) copy-start(s32[1,113]{1,0:T(1,128)} %param.54) | copy-start | bytes 1360
  22.7 53.0 %copy-start.14 = (s32[1,113]{1,0:T(1,128)S(1)}, s32[1,113]{1,0:T(1,128)}, u32[]{:S(2)}) copy-start(s32[1,113]{1,0:T(1,128)} %param.55) | copy-start | bytes 1360
  22.7 53.4 %copy-start.6 = (s32[2,3]{1,0:T(2,128)S(1)}, s32[2,3]{1,0:T(2,128)}, u32[]{:S(2)}) copy-start(s32[2,3]{1,0:T(2,128)} %param.41) | copy-start | bytes 76
  35.5 40.5 %collective-permute-start.3 = (f32[4,2,128]{2,0,1:T(4,128)S(1)}, f32[4,2,128]{2,0,1:T(4,128)S(1)}, u32[]{:S(2)}, u32[]{:S(2)}) collective-permute-start(f32[4,2,128]{2,0,1:T(4,128)S(1)} %convolution_add_fusion.1), channel_id=1, source_target_pairs={{2,0},{4,2},{6,4},{8,6},{10,8},{12,10},{14,12},{16,14},{18,16},{20... | collective-permute-start | bytes 12296 | tf_op jit(solution)/shard_map/ppermute | solution.py:22
  36.8 39.2 %collective-permute-start.2 = (f32[4,2,128]{2,0,1:T(4,128)S(1)}, f32[4,2,128]{2,0,1:T(4,128)S(1)}, u32[]{:S(2)}, u32[]{:S(2)}) collective-permute-start(f32[4,2,128]{2,0,1:T(4,128)S(1)} %convolution_add_fusion.1), channel_id=1, source_target_pairs={{0,2},{2,4},{4,6},{6,8},{8,10},{10,12},{12,14},{14,16},{16,18},{18... | collective-permute-start | bytes 12296 | tf_op jit(solution)/shard_map/ppermute | solution.py:20
  88.0 61.7 %collective-permute-start.5 = (f32[4,2,128]{2,1,0:T(2,128)S(1)}, f32[4,2,128]{2,1,0:T(2,128)S(1)}, u32[]{:S(2)}, u32[]{:S(2)}) collective-permute-start(f32[4,2,128]{2,1,0:T(2,128)S(1)} %all_gather.37), channel_id=1, source_target_pairs={{2,0},{4,2},{6,4},{8,6},{10,8},{12,10},{14,12},{16,14},{18,16},{20... | collective-permute-start | bytes 12296 | tf_op jit(solution)/shard_map/ppermute | solution.py:22
  89.3 60.4 %collective-permute-start.4 = (f32[4,2,128]{2,1,0:T(2,128)S(1)}, f32[4,2,128]{2,1,0:T(2,128)S(1)}, u32[]{:S(2)}, u32[]{:S(2)}) collective-permute-start(f32[4,2,128]{2,1,0:T(2,128)S(1)} %all_gather.37), channel_id=1, source_target_pairs={{0,2},{2,4},{4,6},{6,8},{8,10},{10,12},{12,14},{14,16},{16,18},{18... | collective-permute-start | bytes 12296 | tf_op jit(solution)/shard_map/ppermute | solution.py:20
  180.6 5.0 %collective-permute-start.6 = (f32[1,2,113]{1,2,0:T(8,128)S(1)}, f32[1,2,113]{1,2,0:T(8,128)S(1)}, u32[]{:S(2)}, u32[]{:S(2)}) collective-permute-start(f32[1,2,113]{1,2,0:T(8,128)S(1)} %bitcast.313), channel_id=1, source_target_pairs={{0,2},{2,4},{4,6},{6,8},{8,10},{10,12},{12,14},{14,16},{16,18},{18... | collective-permute-start | bytes 2720 | tf_op jit(solution)/shard_map/ppermute | solution.py:20
  184.3 8.0 %collective-permute-start.7 = (f32[1,2,113]{1,2,0:T(8,128)S(1)}, f32[1,2,113]{1,2,0:T(8,128)S(1)}, u32[]{:S(2)}, u32[]{:S(2)}) collective-permute-start(f32[1,2,113]{1,2,0:T(8,128)S(1)} %bitcast.311), channel_id=1, source_target_pairs={{2,0},{4,2},{6,4},{8,6},{10,8},{12,10},{14,12},{16,14},{18,16},{20... | collective-permute-start | bytes 2720 | tf_op jit(solution)/shard_map/ppermute | solution.py:22
  199.0 36.3 %copy-start.3 = (f32[2,6400]{1,0:T(2,128)S(1)}, f32[2,6400]{1,0:T(2,128)}, u32[]{:S(2)}) copy-start(f32[2,6400]{1,0:T(2,128)} %param.47) | copy-start | bytes 153604
  199.0 36.3 %copy-start.5 = (f32[6400]{0:T(1024)S(1)}, f32[6400]{0:T(1024)}, u32[]{:S(2)}) copy-start(f32[6400]{0:T(1024)} %param.49) | copy-start | bytes 76804
  199.0 241.9 %reduce-scatter.9.cloned.1.call-start = ((), (), s32[]{:S(2)}) async-start(), calls=%async_computation.3 | async-start | bytes 9830400
  247.4 39.1 %collective-permute-start.9 = (f32[4,2,128]{2,0,1:T(4,128)S(1)}, f32[4,2,128]{2,0,1:T(4,128)S(1)}, u32[]{:S(2)}, u32[]{:S(2)}) collective-permute-start(f32[4,2,128]{2,0,1:T(4,128)S(1)} %convolution_add_fusion), channel_id=1, source_target_pairs={{2,0},{4,2},{6,4},{8,6},{10,8},{12,10},{14,12},{16,14},{18,16},{20... | collective-permute-start | bytes 12296 | tf_op jit(solution)/shard_map/ppermute | solution.py:22
  248.7 37.8 %collective-permute-start.8 = (f32[4,2,128]{2,0,1:T(4,128)S(1)}, f32[4,2,128]{2,0,1:T(4,128)S(1)}, u32[]{:S(2)}, u32[]{:S(2)}) collective-permute-start(f32[4,2,128]{2,0,1:T(4,128)S(1)} %convolution_add_fusion), channel_id=1, source_target_pairs={{0,2},{2,4},{4,6},{6,8},{8,10},{10,12},{12,14},{14,16},{16,18},{18... | collective-permute-start | bytes 12296 | tf_op jit(solution)/shard_map/ppermute | solution.py:20
  298.6 60.6 %collective-permute-start.11 = (f32[4,2,128]{2,1,0:T(2,128)S(1)}, f32[4,2,128]{2,1,0:T(2,128)S(1)}, u32[]{:S(2)}, u32[]{:S(2)}) collective-permute-start(f32[4,2,128]{2,1,0:T(2,128)S(1)} %all_gather.42), channel_id=1, source_target_pairs={{2,0},{4,2},{6,4},{8,6},{10,8},{12,10},{14,12},{16,14},{18,16},{20... | collective-permute-start | bytes 12296 | tf_op jit(solution)/shard_map/ppermute | solution.py:22
  300.1 59.2 %collective-permute-start.10 = (f32[4,2,128]{2,1,0:T(2,128)S(1)}, f32[4,2,128]{2,1,0:T(2,128)S(1)}, u32[]{:S(2)}, u32[]{:S(2)}) collective-permute-start(f32[4,2,128]{2,1,0:T(2,128)S(1)} %all_gather.42), channel_id=1, source_target_pairs={{0,2},{2,4},{4,6},{6,8},{8,10},{10,12},{12,14},{14,16},{16,18},{18... | collective-permute-start | bytes 12296 | tf_op jit(solution)/shard_map/ppermute | solution.py:20
  390.4 3.5 collective-permute-start.12
  392.6 8.0 %collective-permute-start.13 = (f32[1,2,113]{1,2,0:T(8,128)S(1)}, f32[1,2,113]{1,2,0:T(8,128)S(1)}, u32[]{:S(2)}, u32[]{:S(2)}) collective-permute-start(f32[1,2,113]{1,2,0:T(8,128)S(1)} %bitcast.312), channel_id=1, source_target_pairs={{2,0},{4,2},{6,4},{8,6},{10,8},{12,10},{14,12},{16,14},{18,16},{20... | collective-permute-start | bytes 2720 | tf_op jit(solution)/shard_map/ppermute | solution.py:22
  (8 other events, 120.3 us)
Sparse Core Ops, SparseCore 0:
  199.1 33.6 reduce-scatter.6
  407.5 33.4 reduce-scatter.8
where the time goes:
time: 452 us; the launch traced here: 451 us
  other arithmetic  152 us (34%)
  local copies, waits for them, and re-layouts  127 us (28%)
  waiting for transfers between devices  63.5 us (14%)
  blocking collectives  33.8 us (7%)
  starting transfers between devices  33.5 us (7%)
  loops' own time  21.4 us (5%)
  between operations  15.4 us (3%)
    scatter-add x2, other arithmetic, shards(): nodal = jnp.zeros(fe_table.shape, jnp.float32).at[:, element_nodes.reshap...  94.8 us
    gather x4, local copies, waits for them, and re-layouts, shards(): disp_el = fe_table[:, element_nodes]  66.9 us
    unnamed x4, waiting for transfers between devices  63.5 us
    scatter-add x4, other arithmetic, shards(): nodal = nodal.at[:, left_ids].add(border[0]).at[:, right_ids].add(border[3])  26.7 us
    ppermute x7, starting transfers between devices, with_halo(): lax.ppermute(tail, axis, [(i, (i + 1) % count) for i in range(ends)])  24.3 us
    gather x4, local copies, waits for them, and re-layouts, shards(): sides = jnp.stack([nodal[:, left_ids], nodal[:, right_ids]])  14 us
    scatter-add x2, other arithmetic, shards(): nodal = nodal.at[:, patch_nodes.reshape(-1)].add(reaction.reshape(2, -1))  13.5 us
    neg x2, other arithmetic, shards(): nodal = -nodal  9.76 us
  transfers between devices with their start and end apart: 16, of which 2 were waited for; matrix products, arithmetic and copies ran while one was open for 44% of the time, Pallas kernels for 0%

commit v1 on v0

v1 whole, which is shorter than its diff:
```python
import functools

import jax
import jax.numpy as jnp
from jax import lax
from jax.experimental import pallas as pl
from jax.experimental.pallas import tpu as pltpu
from jax.sharding import PartitionSpec as P

MESH = pl.DeviceIdType.MESH
F32 = jnp.float32
BF16 = jnp.bfloat16
I32 = jnp.int32
EXACT = lax.Precision.HIGHEST

TIME_STEP = 0.5
CORE_SQ = 0.01
STRETCH = 0.3

LO = 256
HALF_ROWS = 25
PAD_ROWS = 32
CHUNK = 8
N_COPIES = 34


def split2(x):
    top = x.astype(BF16)
    return top, (x - top.astype(F32)).astype(BF16)


def nt(a, b, **kw):
    return lax.dot_general(
        a, b, (((1,), (1,)), ((), ())), preferred_element_type=F32, **kw
    )


def kernel(
    n_dom,
    disp,
    vel,
    coord,
    modulus,
    step,
    family,
    live,
    ptile,
    pblend,
    pnodes,
    pmat,
    fdisp,
    fvel,
    fstep,
    fmod,
    enodes,
    sgrad,
    qweight,
    sleft,
    sright,
    disp_out,
    vel_out,
    fdisp_out,
    fvel_out,
    pdx,
    ub0,
    ub1,
    st0,
    st1,
    pm,
    table,
    speed,
    split_table,
    onehot,
    hrow,
    ids,
    link,
    del_,
    fel,
    sgt,
    acc,
    bonds,
    sums,
    cur,
    pel_send,
    pel_recv,
    late_send,
    late_recv,
    bd_send,
    bd_recv,
    ssem,
    rsem,
):
    d = lax.axis_index("dom")
    b = lax.axis_index("blk")
    o = 1 - b
    left = lax.rem(d + n_dom - 1, n_dom)
    right = lax.rem(d + 1, n_dom)
    peers = ((d, o), (left, 0), (left, 1), (right, 0), (right, 1))

    barrier = pltpu.get_barrier_semaphore()
    for peer in peers:
        pl.semaphore_signal(barrier, inc=1, device_id=peer, device_id_type=MESH)

    started = []

    def send(src, dst, ssem_at, rsem_at, peer):
        copy = pltpu.make_async_remote_copy(
            src_ref=src,
            dst_ref=dst,
            send_sem=ssem.at[ssem_at],
            recv_sem=rsem.at[rsem_at],
            device_id=peer,
            device_id_type=MESH,
        )
        copy.start()
        started.append(copy)

    def arrived(dst, rsem_at):
        pltpu.make_async_remote_copy(
            src_ref=dst,
            dst_ref=dst,
            send_sem=ssem.at[0],
            recv_sem=rsem.at[rsem_at],
            device_id=(d, o),
            device_id_type=MESH,
        ).wait_recv()

    own = 4 + 2 * b
    theirs = 4 + 2 * o

    for t in range(2):
        pdx[own + t] = jnp.concatenate(
            [
                coord[t],
                modulus[t : t + 1, :],
                disp[t],
                pnodes[...].astype(F32),
                jnp.zeros((2, 128), F32),
            ],
            axis=0,
        )
    table[b, 24:32, :] = jnp.zeros((8, LO), F32)
    table[b, 56:64, :] = jnp.zeros((8, LO), F32)
    for r in range(HALF_ROWS):
        lanes = slice(r * LO, (r + 1) * LO)
        table[b, r : r + 1, :] = fdisp[0:1, lanes]
        table[b, PAD_ROWS + r : PAD_ROWS + r + 1, :] = fdisp[1:2, lanes]
    pl.semaphore_wait(barrier, 5)

    send(table.at[b], table.at[b], 0, 0, (d, o))
    slots = (own, 8 + 2 * b, 8 + 2 * b, 2 * b, 2 * b)
    marks = (0, 3 + b, 3 + b, 1 + b, 1 + b)
    for j in range(5):
        send(
            pdx.at[pl.ds(own, 2)],
            pdx.at[pl.ds(slots[j], 2)],
            3 + j,
            3 + marks[j],
            peers[j],
        )
    send(pmat.at[0], pm.at[b], 1, 1, (d, o))
    sources = (theirs, 0, 2, 8, 10)

    speed[b, 24:32, :] = jnp.zeros((8, LO), F32)
    speed[b, 56:64, :] = jnp.zeros((8, LO), F32)
    speed[b, 88:96, :] = jnp.zeros((8, LO), F32)
    for r in range(HALF_ROWS):
        lanes = slice(r * LO, (r + 1) * LO)
        speed[b, r : r + 1, :] = fvel[0:1, lanes]
        speed[b, PAD_ROWS + r : PAD_ROWS + r + 1, :] = fvel[1:2, lanes]
        speed[b, 2 * PAD_ROWS + r : 2 * PAD_ROWS + r + 1, :] = fstep[0:1, lanes]
    send(speed.at[b], speed.at[b], 2, 2, (d, o))
    pm[b] = pmat[0]
    states = (started[0], started.pop())
    del started[0]

    lo_iota = lax.broadcasted_iota(I32, (LO, 128), 0)

    def table_row(node):
        hi = lax.shift_right_arithmetic(node, 8)
        return jnp.where(hi >= HALF_ROWS, hi + (PAD_ROWS - HALF_ROWS), hi)

    def onehot_of(lo_row):
        return jnp.where(
            lo_iota == jnp.broadcast_to(lo_row, (LO, 128)), 1.0, 0.0
        ).astype(BF16)

    @pl.loop(0, 64 // CHUNK)
    def _(i):
        node = enodes[pl.ds(pl.multiple_of(i * CHUNK, CHUNK), CHUNK), :]
        hrow[pl.ds(pl.multiple_of(i * CHUNK, CHUNK), CHUNK), :] = table_row(node)
        lo = lax.bitwise_and(node, LO - 1)
        base = pl.multiple_of(i * (CHUNK * 128), CHUNK * 128)
        for g in range(CHUNK):
            onehot[:, pl.ds(base + g * 128, 128)] = onehot_of(lo[g : g + 1, :])

    sgt[...] = sgrad[...].T
    eye = lax.broadcasted_iota(I32, (64, 64), 0) == lax.broadcasted_iota(
        I32, (64, 64), 1
    )
    weight = jnp.sum(
        jnp.where(eye, jnp.broadcast_to(qweight[...], (64, 64)), 0.0),
        axis=1,
        keepdims=True,
    )
    scale = weight * fmod[...]

    for j in range(5):
        arrived(pdx.at[pl.ds(sources[j], 2)], 3 + j)

    ids[...] = jnp.full((8, 128), -1, I32)
    ids[pl.ds(b, 1), :] = pnodes[...]
    ids[pl.ds(o, 1), :] = pdx[theirs, 5:6, :].astype(I32)
    ids[2:3, 0:113] = sleft[...]
    ids[3:4, 0:113] = sright[...]
    few = ids[...]
    hrow[64:72, :] = table_row(few)
    few_lo = lax.bitwise_and(few, LO - 1)
    for g in range(4):
        onehot[:, 8192 + g * 128 : 8320 + g * 128] = onehot_of(few_lo[g : g + 1, :])
    few_f = few.astype(F32)
    few_t = few_f.T
    for q in range(2):
        for side in range(2):
            link[q * 128 : (q + 1) * 128, side * 128 : (side + 1) * 128] = jnp.where(
                few_t[:, q : q + 1] == few_f[2 + side : 3 + side, :], 1.0, 0.0
            ).astype(BF16)

    OX, OY, REST, INFL0, NX, NY, STR, INFL = range(8)

    @pl.loop(0, 6)
    def _(p):
        t = p // 3
        far = pdx[family[t, p - 3 * t]]
        far_t = far.T
        me = pdx[own + t]
        ox = far_t[:, 0:1] - me[0:1, :]
        oy = far_t[:, 1:2] - me[1:2, :]
        r2 = ox * ox + oy * oy
        bonds[OX, p] = ox
        bonds[OY, p] = oy
        bonds[REST, p] = jnp.sqrt(r2 + CORE_SQ)
        bonds[INFL0, p] = jnp.exp(-0.5 * r2)

    cur[...] = vel[...]
    row_iota = lax.broadcasted_iota(I32, (64, 128), 0)

    def masked_rows(product, row):
        both = product[0:128] + product[128:256]
        hit = row_iota == jnp.broadcast_to(row, (64, 128))
        out = []
        for c in range(2):
            x = jnp.where(hit[0:32], both[c * 32 : c * 32 + 32], 0.0)
            x = x + jnp.where(hit[32:64], both[64 + c * 32 : 96 + c * 32], 0.0)
            out.append(jnp.sum(x, axis=0, keepdims=True))
        return out

    def spread(values, row):
        hit = row_iota == jnp.broadcast_to(row, (64, 128))
        blocks = []
        for part in range(2):
            wide = [
                jnp.where(hit, jnp.broadcast_to(values[part][c], (64, 128)), 0.0)
                for c in range(2)
            ]
            for half in range(2):
                for c in range(2):
                    blocks.append(wide[c][half * 32 : half * 32 + 32])
        return jnp.concatenate(blocks, axis=0).astype(BF16)

    for s in range(2):
        ub, st = (ub0, ub1)[s], (st0, st1)[s]
        base = 8 + 13 * s
        if s == 0:
            arrived(table.at[o], 0)
            arrived(pm.at[o], 1)

        top, low = split2(table[...].reshape(128, LO))
        split_table[0:128, :] = top
        split_table[128:256, :] = low
        product = jnp.dot(
            split_table[...], onehot[:, 8192:8448], preferred_element_type=F32
        )
        targets = []
        for q in range(2):
            picked = masked_rows(
                product[:, q * 128 : (q + 1) * 128], hrow[64 + q : 65 + q, :]
            )
            picked = jnp.concatenate(picked + [jnp.zeros((6, 128), F32)], axis=0)
            targets.append(nt(picked, pm[q], precision=EXACT)[0:2, :])
        for k in range(4):
            if s == 0:
                u = pdx[4 + k, 3:5, :]
            else:
                t = k % 2
                mine = ub[4 + k]
                u = mine
            new = u
            for q in range(2):
                hit = jnp.full((2, 128), ptile[q], I32) == k
                new = jnp.where(
                    hit, u + pblend[q : q + 1, :] * (targets[q] - u), new
                )
            ub[4 + k] = new
        send(ub.at[pl.ds(4, 4)], ub.at[pl.ds(8, 4)], base, base + 1, (left, b))
        send(ub.at[pl.ds(4, 4)], ub.at[pl.ds(0, 4)], base + 1, base, (right, b))

        @pl.loop(0, 64 // CHUNK)
        def _(i):
            rows = pl.ds(pl.multiple_of(i * CHUNK, CHUNK), CHUNK)
            lanes = pl.ds(pl.multiple_of(i * (CHUNK * 128), CHUNK * 128), CHUNK * 128)
            product = jnp.dot(
                split_table[...], onehot[:, lanes], preferred_element_type=F32
            )
            row = hrow[rows, :]
            found = [
                masked_rows(product[:, g * 128 : (g + 1) * 128], row[g : g + 1, :])
                for g in range(CHUNK)
            ]
            for c in range(2):
                del_[rows, c * 128 : (c + 1) * 128] = jnp.concatenate(
                    [f[c] for f in found], axis=0
                )

        arrived(ub.at[pl.ds(0, 4)], base)
        arrived(ub.at[pl.ds(8, 4)], base + 1)

        @pl.loop(0, 6)
        def _(p):
            t = p // 3
            far = ub[family[t, p - 3 * t]]
            far_t = jnp.concatenate([far, jnp.zeros((6, 128), F32)], axis=0).T
            me = ub[own + t]
            yx = bonds[OX, p] + (far_t[:, 0:1] - me[0:1, :])
            yy = bonds[OY, p] + (far_t[:, 1:2] - me[1:2, :])
            y2 = yx * yx + yy * yy + CORE_SQ
            length = jnp.sqrt(y2)
            inverse = 1.0 / length
            rest = bonds[REST, p]
            stretch = length - rest
            ratio = stretch * (1.0 / STRETCH)
            influence = bonds[INFL0, p] / (1.0 + ratio * ratio)
            bonds[NX, p] = yx * inverse
            bonds[NY, p] = yy * inverse
            bonds[STR, p] = stretch
            bonds[INFL, p] = influence
            weighted = influence * rest
            sums[p] = jnp.concatenate(
                [
                    jnp.sum(weighted * stretch, axis=0, keepdims=True),
                    jnp.sum(weighted * rest, axis=0, keepdims=True),
                ],
                axis=0,
            )

        for t in range(2):
            total = sums[3 * t] + sums[3 * t + 1] + sums[3 * t + 2]
            volume = total[1:2, :]
            st[own + t] = jnp.concatenate(
                [2.0 * total[0:1, :] / volume, volume], axis=0
            )
        for j in range(5):
            send(
                st.at[pl.ds(own, 2)],
                st.at[pl.ds(slots[j], 2)],
                base + 2 + j,
                base + 2 + marks[j],
                peers[j],
            )

        grad = jnp.dot(sgrad[...], del_[...], precision=EXACT, preferred_element_type=F32)
        exx = grad[0:64, 0:128]
        eyy = grad[64:128, 128:256]
        exy = 0.5 * (grad[64:128, 0:128] + grad[0:64, 128:256])
        scaled = scale * (1.0 + exx * exx + eyy * eyy + 2.0 * exy * exy)
        both = exx + eyy
        sxx = scaled * (both + 2.0 * exx)
        syy = scaled * (both + 2.0 * eyy)
        sxy = scaled * 2.0 * exy
        stress = jnp.concatenate(
            [
                jnp.concatenate([sxx, sxy], axis=1),
                jnp.concatenate([sxy, syy], axis=1),
            ],
            axis=0,
        )
        fel[...] = jnp.dot(sgt[...], stress, precision=EXACT, preferred_element_type=F32)
        acc[...] = jnp.zeros((256, LO), F32)

        @pl.loop(0, 64 // CHUNK)
        def _(i):
            rows = pl.ds(pl.multiple_of(i * CHUNK, CHUNK), CHUNK)
            lanes = pl.ds(pl.multiple_of(i * (CHUNK * 128), CHUNK * 128), CHUNK * 128)
            row = hrow[rows, :]
            f = fel[rows, :]
            f_top = f.astype(BF16).astype(F32)
            f_low = f - f_top
            left_side = jnp.concatenate(
                [
                    spread(
                        [
                            [x[g : g + 1, 0:128], x[g : g + 1, 128:256]]
                            for x in (f_top, f_low)
                        ],
                        row[g : g + 1, :],
                    )
                    for g in range(CHUNK)
                ],
                axis=1,
            )
            acc[...] += nt(left_side, onehot[:, lanes])

        partial = acc[0:128, :] + acc[128:256, :]
        pel_send[s] = partial
        if s == 0:
            send(pel_send.at[s], pel_recv.at[s], base + 7, base + 7, (d, o))
        else:
            cut = pl.ds(o * 64, 64)
            send(
                pel_send.at[s, cut], pel_recv.at[s, cut], base + 7, base + 7, (d, o)
            )
        top, low = split2(partial)
        product = jnp.dot(
            jnp.concatenate([top, low], axis=0),
            onehot[:, 8448:8704],
            preferred_element_type=F32,
        )
        border = []
        for side in range(2):
            found = masked_rows(
                product[:, side * 128 : (side + 1) * 128],
                hrow[66 + side : 67 + side, :],
            )
            border.append(jnp.concatenate(found, axis=0))

        for j in range(5):
            arrived(st.at[pl.ds(sources[j], 2)], base + 2 + j)

        def coefficients(k, state):
            theta, volume = state[0:1, :], state[1:2, :]
            return 2.0 * k * theta / volume, 4.0 * k / volume, 0.5 * theta

        @pl.loop(0, 6)
        def _(p):
            t = p // 3
            j = family[t, p - 3 * t]
            fa, fb, fc = coefficients(pdx[j][2:3, :], st[j])
            far_t = jnp.concatenate([fa, fb, fc, jnp.zeros((5, 128), F32)], axis=0).T
            oa, ob, oc = coefficients(pdx[own + t][2:3, :], st[own + t])
            rest = bonds[REST, p]
            stretch = bonds[STR, p]
            near = oa * rest + ob * (stretch - oc * rest)
            away = far_t[:, 0:1] * rest + far_t[:, 1:2] * (stretch - far_t[:, 2:3] * rest)
            force = bonds[INFL, p] * (near + away)
            sums[p] = jnp.concatenate(
                [
                    jnp.sum(force * bonds[NX, p], axis=0, keepdims=True),
                    jnp.sum(force * bonds[NY, p], axis=0, keepdims=True),
                ],
                axis=0,
            )

        forces, moved = [], []
        for t in range(2):
            alive = jnp.full((2, 128), 2 * b + t, I32) < live[0]
            total = sums[3 * t] + sums[3 * t + 1] + sums[3 * t + 2]
            force = jnp.where(alive, total, 0.0)
            forces.append(force)
            v = jnp.where(alive, cur[t] + step[t : t + 1, :] * force, 0.0)
            u = jnp.where(alive, ub[own + t] + TIME_STEP * v, 0.0)
            cur[t] = v
            moved.append(u)

        reaction = []
        for q in range(2):
            w = jnp.zeros((2, 128), F32)
            for t in range(2):
                hit = jnp.full((2, 128), ptile[q], I32) == 2 * b + t
                w = w + jnp.where(hit, pblend[q : q + 1, :] * forces[t], 0.0)
            w = jnp.concatenate([w, jnp.zeros((6, 128), F32)], axis=0)
            reaction.append(
                jnp.dot(w, pm[q], precision=EXACT, preferred_element_type=F32)[0:2, :]
            )
        late = jnp.concatenate(reaction + moved, axis=0)
        late_send[s] = late
        send(late_send.at[s], late_recv.at[s], base + 8, base + 8, (d, o))
        wide = jnp.concatenate(reaction, axis=1)
        top, low = split2(wide)
        met = jnp.dot(
            jnp.concatenate([top, low, jnp.zeros((12, 256), BF16)], axis=0),
            link[...],
            preferred_element_type=F32,
        )
        met = met[0:2, :] + met[2:4, :]
        for side in range(2):
            bd_send[s, side] = met[:, side * 128 : (side + 1) * 128] - border[side]
        for j in range(4):
            side = j // 2
            send(
                bd_send.at[s, side],
                bd_recv.at[s, 2 * (1 - side) + b],
                base + 9 + j,
                base + 9 + 2 * (1 - side) + b,
                peers[1 + j],
            )
        if s == 0:
            for t in range(2):
                ub1[own + t] = moved[t]
        else:
            for t in range(2):
                disp_out[t] = moved[t]
                vel_out[t] = cur[t]

        arrived(late_recv.at[s], base + 8)
        other = late_recv[s]
        if s == 0:
            for t in range(2):
                ub1[theirs + t] = other[4 + 2 * t : 6 + 2 * t, :]
        for j in range(4):
            arrived(bd_recv.at[s, j], base + 9 + j)
        shared = [
            jnp.where(
                jnp.full((2, 128), d, I32) > 0, bd_recv[s, 0] + bd_recv[s, 1], 0.0
            ),
            jnp.where(
                jnp.full((2, 128), d, I32) < n_dom - 1,
                bd_recv[s, 2] + bd_recv[s, 3],
                0.0,
            ),
        ]
        sides = []
        for g, x in enumerate(
            [late[0:2, :] + other[0:2, :], late[2:4, :] + other[2:4, :]] + shared
        ):
            x_top = x.astype(BF16).astype(F32)
            x_low = x - x_top
            sides.append(
                spread(
                    [[y[0:1, :], y[1:2, :]] for y in (x_top, x_low)],
                    hrow[64 + g : 65 + g, :],
                )
            )
        extra = nt(jnp.concatenate(sides, axis=1), onehot[:, 8192:8704])
        acc[0:128, :] = extra[0:128, :] + extra[128:256, :]
        if s == 0:
            arrived(speed.at[o], 2)
            arrived(pel_recv.at[s], base + 7)
            for copy in states:
                copy.wait_send()
        else:
            arrived(pel_recv.at[s, pl.ds(b * 64, 64)], base + 7)
        for h in range(2) if s == 0 else (b,):
            for c in range(2):
                cut = pl.ds(h * 64 + c * 32, 32)
                rows = slice(c * 32, c * 32 + 32)
                nodal = acc[cut, :] - (pel_send[s, cut, :] + pel_recv[s, cut, :])
                v = speed[h, rows, :] + speed[h, 64:96, :] * nodal
                speed[h, rows, :] = v
                table[h, rows, :] = table[h, rows, :] + TIME_STEP * v

    for r in range(HALF_ROWS):
        lanes = slice(r * LO, (r + 1) * LO)
        for c in range(2):
            at = PAD_ROWS * c + r
            fdisp_out[c : c + 1, lanes] = table[b, at : at + 1, :]
            fvel_out[c : c + 1, lanes] = speed[b, at : at + 1, :]
    for copy in started:
        copy.wait_send()


def shards(n_dom, *args):
    (
        pd_disp,
        pd_vel,
        pd_coord,
        pd_modulus,
        pd_step,
        family,
        live,
        patch_tile,
        patch_blend,
        patch_nodes,
        patch_matrix,
        fe_disp,
        fe_vel,
        fe_step,
        fe_modulus,
        element_nodes,
        shape_grad,
        quad_weight,
        shared_left,
        shared_right,
    ) = args
    vmem = pl.BlockSpec(memory_space=pltpu.VMEM)
    smem = pl.BlockSpec(memory_space=pltpu.SMEM)
    in_specs = [vmem] * 20
    for at in (5, 6, 7):
        in_specs[at] = smem

    def f32(*shape):
        return pltpu.VMEM(shape, F32)

    return pl.pallas_call(
        functools.partial(kernel, n_dom),
        out_shape=[
            jax.ShapeDtypeStruct(pd_disp.shape, F32),
            jax.ShapeDtypeStruct(pd_vel.shape, F32),
            jax.ShapeDtypeStruct(fe_disp.shape, F32),
            jax.ShapeDtypeStruct(fe_vel.shape, F32),
        ],
        in_specs=in_specs,
        out_specs=[vmem] * 4,
        scratch_shapes=[
            f32(12, 8, 128),
            f32(12, 2, 128),
            f32(12, 2, 128),
            f32(12, 2, 128),
            f32(12, 2, 128),
            f32(2, 128, 128),
            f32(2, 64, LO),
            f32(2, 96, LO),
            pltpu.VMEM((256, LO), BF16),
            pltpu.VMEM((LO, 8704), BF16),
            pltpu.VMEM((72, 128), I32),
            pltpu.VMEM((8, 128), I32),
            pltpu.VMEM((256, 256), BF16),
            f32(64, 256),
            f32(64, 256),
            f32(64, 128),
            f32(256, LO),
            f32(8, 6, 128, 128),
            f32(6, 2, 128),
            f32(2, 2, 128),
            f32(2, 128, LO),
            f32(2, 128, LO),
            f32(2, 8, 128),
            f32(2, 8, 128),
            f32(2, 2, 2, 128),
            f32(2, 4, 2, 128),
            pltpu.SemaphoreType.DMA((N_COPIES,)),
            pltpu.SemaphoreType.DMA((N_COPIES,)),
        ],
        compiler_params=pltpu.CompilerParams(
            collective_id=0, has_side_effects=True, vmem_limit_bytes=40 * 2**20
        ),
    )(
        pd_disp,
        pd_vel,
        pd_coord,
        pd_modulus,
        pd_step,
        family,
        live,
        patch_tile,
        patch_blend,
        patch_nodes,
        patch_matrix,
        fe_disp,
        fe_vel,
        fe_step.reshape(1, -1),
        fe_modulus.reshape(1, -1),
        element_nodes,
        shape_grad.reshape(-1, shape_grad.shape[2]),
        quad_weight.reshape(1, -1),
        shared_left,
        shared_right,
    )


def solution(mesh):
    both = ("dom", "blk")
    return jax.shard_map(
        functools.partial(shards, mesh.shape["dom"]),
        mesh=mesh,
        in_specs=(
            P(both, None, None),
            P(both, None, None),
            P(both, None, None),
            P(both, None),
            P(both, None),
            P(both, None),
            P("dom"),
            P("dom"),
            P("dom", None),
            P(both, None),
            P(both, None, None),
            P(None, both),
            P(None, both),
            P(both),
            P(both),
            P(None, both),
            P(),
            P(),
            P("dom", None),
            P("dom", None),
        ),
        out_specs=(
            P(both, None, None),
            P(both, None, None),
            P(None, both),
            P(None, both),
        ),
        check_vma=False,
    )
```

time: 452 us -> 74.6 us (0.17)
  other arithmetic: 152 us -> 0 us
  local copies, waits for them, and re-layouts: 127 us -> 9.76 us
  waiting for transfers between devices: 63.5 us -> 0 us
  Pallas kernels: 0 us -> 62.9 us
  blocking collectives: 33.8 us -> 0 us
  starting transfers between devices: 33.5 us -> 0 us
  loops' own time: 21.4 us -> 0 us
  between operations: 15.4 us -> 1.46 us
    scatter-add x8 -> x0, other arithmetic: 135 us -> none  [the longest x2 94.8 us: shards(): nodal = jnp.zeros(fe_table.shape, jnp.float32).at[:, element_nodes.reshap...]
    gather x38 -> x0, local copies, waits for them, and re-layouts: 104 us -> none  [the longest x4 66.9 us: shards(): disp_el = fe_table[:, element_nodes]]
    unnamed x4 -> x0, waiting for transfers between devices: 63.5 us -> none
    pallas_call x0 -> x1, Pallas kernels: none -> 62.9 us  [shards(): pl.pallas_call(functools.partial(kernel, n_dom), out_shape=[jax.ShapeDtyp...]
    all_gather x11 -> x0, blocking collectives: 33.8 us -> none  [the longest x2 8.64 us: shards(): fe_table = lax.all_gather(fe_disp, 'blk', axis=1, tiled=True)]
    ppermute x14 -> x0, starting transfers between devices: 33.5 us -> none  [the longest x7 24.3 us: with_halo(): lax.ppermute(tail, axis, [(i, (i + 1) % count) for i in range(ends)])]
    another operation x12 -> x0, loops' own time: 21.4 us -> none  [the longest x4 5.53 us: force_one(): return lax.cond(tile_number < active_flags, force_run, force_skip, None)]
    neg x2 -> x0, other arithmetic: 9.76 us -> none  [shards(): nodal = -nodal]
  transfers between devices with their start and end apart: 16 -> 0, of which waited for: 2 -> 0; matrix products, arithmetic and copies ran while one was open for 44% -> 0% of each run, Pallas kernels for 0% -> 0%
where the time goes in v1:
time: 74.6 us; the launch traced here: 74.1 us
  Pallas kernels  62.9 us (84%)
  local copies, waits for them, and re-layouts  9.76 us (13%)
  between operations  1.46 us (2%)
    pallas_call x1, Pallas kernels, shards(): pl.pallas_call(functools.partial(kernel, n_dom), out_shape=[jax.ShapeDtyp...  62.9 us
    unnamed x40, local copies, waits for them, and re-layouts  8.94 us

profile of v1, /device:TPU:1, one launch (start us, length us, event | category | flops | bytes accessed | tf_op | source)
XLA Modules:
  0.0 74.1 jit_solution(9143921085967665144)
XLA Ops:
  0.6 0.0 copy-start.2
  1.3 0.0 copy-start.5
  1.3 0.0 copy-start.6
  1.3 0.0 copy-start.7
  1.3 0.0 copy-start.8
  1.3 0.0 copy-start.9
  1.3 0.0 copy-start.10
  1.4 0.0 copy-start.11
  1.4 0.8 %reshape.20.fstep = f32[1,6400]{1,0:T(1,128)S(1)} reshape(f32[6400]{0:T(1024)} %param.33) | data formatting | bytes 51200 | tf_op jit(solution)/shard_map/reshape | solution.py:660
  2.3 0.0 copy-start
  2.3 0.8 %copy-done = f32[1,128,128]{2,1,0:T(8,128)S(1)} copy-done((f32[1,128,128]{2,1,0:T(8,128)S(1)}, f32[1,128,128]{2,1,0:T(8,128)}, u32[]{:S(2)}) %copy-start) | copy-done | bytes 65560
  3.1 0.8 %copy-done.1 = f32[2,64,64]{2,1,0:T(8,128)S(1)} copy-done((f32[2,64,64]{2,1,0:T(8,128)S(1)}, f32[2,64,64]{2,1,0:T(8,128)}, u32[]{:S(2)}) %copy-start.1) | copy-done | bytes 32792
  4.0 0.8 %copy-done.3 = f32[2,6400]{1,0:T(2,128)S(1)} copy-done((f32[2,6400]{1,0:T(2,128)S(1)}, f32[2,6400]{1,0:T(2,128)}, u32[]{:S(2)}) %copy-start.3) | copy-done | bytes 51224
  4.8 0.8 %copy-done.4 = s32[64,128]{1,0:T(8,128)S(1)} copy-done((s32[64,128]{1,0:T(8,128)S(1)}, s32[64,128]{1,0:T(8,128)}, u32[]{:S(2)}) %copy-start.4) | copy-done | bytes 32792
  5.5 0.7 copy-done.13
  6.2 0.7 copy-done.14
  6.8 0.7 copy-done.15
  7.5 0.7 copy-done.16
  8.2 0.7 copy-done.17
  8.8 62.9 %shard_map.219 = (f32[2,2,128]{2,1,0:T(2,128)S(1)}, f32[2,2,128]{2,1,0:T(2,128)S(1)}, f32[2,6400]{1,0:T(2,128)S(1)}, f32[2,6400]{1,0:T(2,128)S(1)}) custom-call(f32[2,2,128]{2,1,0:T(2,128)S(1)} %copy-done.5, f32[2,2,128]{2,1,0:T(2,128)S(1)} %copy-done.6, f32[2,2,128]{2,1,0:T(2,128)S(1)} %copy-done.7, f32[2,128]{1,0:T(2,128)S(1)} %copy-done.8, ...), custom_call_target="tpu_custom_call" | custom-call | tf_op jit(solution)/shard_map/pallas_call | solution.py:603
  71.7 0.6 copy.29
  72.3 0.6 copy.30
  72.9 0.6 copy.31
  73.5 0.6 copy.32
  (18 shorter events, 0.0 us)
Async XLA Ops:
  0.6 1.6 %copy-start.2 = (f32[2,6400]{1,0:T(2,128)S(1)}, f32[2,6400]{1,0:T(2,128)}, u32[]{:S(2)}) copy-start(f32[2,6400]{1,0:T(2,128)} %fdisp.1) | copy-start | bytes 153604
  1.3 0.9 %copy-start.5 = (f32[2,2,128]{2,1,0:T(2,128)S(1)}, f32[2,2,128]{2,1,0:T(2,128)}, u32[]{:S(2)}) copy-start(f32[2,2,128]{2,1,0:T(2,128)} %disp.1) | copy-start | bytes 6148
  1.3 0.9 %copy-start.6 = (f32[2,2,128]{2,1,0:T(2,128)S(1)}, f32[2,2,128]{2,1,0:T(2,128)}, u32[]{:S(2)}) copy-start(f32[2,2,128]{2,1,0:T(2,128)} %vel.1) | copy-start | bytes 6148
  1.3 0.9 %copy-start.7 = (f32[2,2,128]{2,1,0:T(2,128)S(1)}, f32[2,2,128]{2,1,0:T(2,128)}, u32[]{:S(2)}) copy-start(f32[2,2,128]{2,1,0:T(2,128)} %coord.1) | copy-start | bytes 6148
  1.3 0.9 %copy-start.8 = (f32[2,128]{1,0:T(2,128)S(1)}, f32[2,128]{1,0:T(2,128)}, u32[]{:S(2)}) copy-start(f32[2,128]{1,0:T(2,128)} %modulus.1) | copy-start | bytes 3076
  1.3 0.9 %copy-start.9 = (f32[2,128]{1,0:T(2,128)S(1)}, f32[2,128]{1,0:T(2,128)}, u32[]{:S(2)}) copy-start(f32[2,128]{1,0:T(2,128)} %step.1) | copy-start | bytes 3076
  1.3 0.9 %copy-start.10 = (s32[2,3]{1,0:T(2,128)S(1)}, s32[2,3]{1,0:T(2,128)}, u32[]{:S(2)}) copy-start(s32[2,3]{1,0:T(2,128)} %family.1) | copy-start | bytes 76
  1.4 0.9 %copy-start.11 = (f32[2,128]{1,0:T(2,128)S(1)}, f32[2,128]{1,0:T(2,128)}, u32[]{:S(2)}) copy-start(f32[2,128]{1,0:T(2,128)} %pblend.1) | copy-start | bytes 3076
  1.4 0.9 %copy-start.12 = (s32[2]{0:T(128)S(1)}, s32[2]{0:T(128)}, u32[]{:S(2)}) copy-start(s32[2]{0:T(128)} %ptile.1) | copy-start | bytes 28
  2.3 0.8 %copy-start = (f32[1,128,128]{2,1,0:T(8,128)S(1)}, f32[1,128,128]{2,1,0:T(8,128)}, u32[]{:S(2)}) copy-start(f32[1,128,128]{2,1,0:T(8,128)} %pmat.1) | copy-start | bytes 196612
  3.1 0.8 %copy-start.1 = (f32[2,64,64]{2,1,0:T(8,128)S(1)}, f32[2,64,64]{2,1,0:T(8,128)}, u32[]{:S(2)}) copy-start(f32[2,64,64]{2,1,0:T(8,128)} %param.36) | copy-start | bytes 98308
  4.0 0.8 %copy-start.3 = (f32[2,6400]{1,0:T(2,128)S(1)}, f32[2,6400]{1,0:T(2,128)}, u32[]{:S(2)}) copy-start(f32[2,6400]{1,0:T(2,128)} %fvel.1) | copy-start | bytes 153604
  4.8 0.8 %copy-start.4 = (s32[64,128]{1,0:T(8,128)S(1)}, s32[64,128]{1,0:T(8,128)}, u32[]{:S(2)}) copy-start(s32[64,128]{1,0:T(8,128)} %enodes.1) | copy-start | bytes 98308
  5.5 0.7 copy-start.13
  6.2 0.7 copy-start.14
  6.8 0.7 copy-start.15
  7.5 0.7 copy-start.16
  8.2 0.7 copy-start.17

commit v2 on v1

--- a/solution.py
+++ b/solution.py
@@ -22,6 +22,7 @@
 PAD_ROWS = 32
 CHUNK = 8
 N_COPIES = 34
+VMEM_BYTES = 60 * 2**20
 
 
 def split2(x):
@@ -37,6 +38,30 @@
 
 def kernel(
     n_dom,
+    disp_in,
+    vel_in,
+    coord_in,
+    modulus_in,
+    step_in,
+    family_in,
+    live_in,
+    ptile_in,
+    pblend_in,
+    pnodes_in,
+    pmat_in,
+    fdisp_in,
+    fvel_in,
+    fstep_in,
+    fmod_in,
+    enodes_in,
+    sgrad_in,
+    qweight_in,
+    sleft_in,
+    sright_in,
+    disp_out,
+    vel_out,
+    fdisp_out,
+    fvel_out,
     disp,
     vel,
     coord,
@@ -47,7 +72,6 @@
     ptile,
     pblend,
     pnodes,
-    pmat,
     fdisp,
     fvel,
     fstep,
@@ -57,10 +81,6 @@
     qweight,
     sleft,
     sright,
-    disp_out,
-    vel_out,
-    fdisp_out,
-    fvel_out,
     pdx,
     ub0,
     ub1,
@@ -89,21 +109,72 @@
     bd_recv,
     ssem,
     rsem,
+    lsem,
 ):
     d = lax.axis_index("dom")
     b = lax.axis_index("blk")
     o = 1 - b
-    left = lax.rem(d + n_dom - 1, n_dom)
-    right = lax.rem(d + 1, n_dom)
+    has_left = d > 0
+    has_right = d < n_dom - 1
+    left = jnp.maximum(d - 1, 0)
+    right = jnp.minimum(d + 1, n_dom - 1)
     peers = ((d, o), (left, 0), (left, 1), (right, 0), (right, 1))
+    there = (None, has_left, has_left, has_right, has_right)
+
+    def if_there(cond, act):
+        if cond is None:
+            act()
+        else:
+            pl.when(cond)(act)
 
     barrier = pltpu.get_barrier_semaphore()
-    for peer in peers:
-        pl.semaphore_signal(barrier, inc=1, device_id=peer, device_id_type=MESH)
+    for peer, cond in zip(peers, there):
+        if_there(
+            cond,
+            functools.partial(
+                pl.semaphore_signal,
+                barrier,
+                inc=1,
+                device_id=peer,
+                device_id_type=MESH,
+            ),
+        )
+
+    loads = {}
+    for at, (src, dst) in enumerate(
+        (
+            (fdisp_in, fdisp),
+            (coord_in, coord),
+            (modulus_in, modulus),
+            (disp_in, disp),
+            (pnodes_in, pnodes),
+            (pmat_in.at[0], pm.at[b]),
+            (fvel_in, fvel),
+            (fstep_in, fstep),
+            (enodes_in, enodes),
+            (vel_in, vel),
+            (step_in, step),
+            (family_in, family),
+            (live_in, live),
+            (ptile_in, ptile),
+            (pblend_in, pblend),
+            (fmod_in, fmod),
+            (sgrad_in, sgrad),
+            (qweight_in, qweight),
+            (sleft_in, sleft),
+            (sright_in, sright),
+        )
+    ):
+        loads[at] = pltpu.make_async_copy(src, dst, lsem.at[at])
+        loads[at].start()
+
+    def loaded(*which):
+        for at in which:
+            loads[at].wait()
 
     started = []
 
-    def send(src, dst, ssem_at, rsem_at, peer):
+    def send(src, dst, ssem_at, rsem_at, peer, cond):
         copy = pltpu.make_async_remote_copy(
             src_ref=src,
             dst_ref=dst,
@@ -112,22 +183,24 @@
             device_id=peer,
             device_id_type=MESH,
         )
-        copy.start()
-        started.append(copy)
-
-    def arrived(dst, rsem_at):
-        pltpu.make_async_remote_copy(
+        if_there(cond, copy.start)
+        started.append((copy, cond))
+
+    def arrived(dst, rsem_at, cond):
+        copy = pltpu.make_async_remote_copy(
             src_ref=dst,
             dst_ref=dst,
             send_sem=ssem.at[0],
             recv_sem=rsem.at[rsem_at],
             device_id=(d, o),
             device_id_type=MESH,
-        ).wait_recv()
+        )
+        if_there(cond, copy.wait_recv)
 
     own = 4 + 2 * b
     theirs = 4 + 2 * o
 
+    loaded(1, 2, 3, 4)
     for t in range(2):
         pdx[own + t] = jnp.concatenate(
             [
@@ -139,15 +212,18 @@
             ],
             axis=0,
         )
+    loaded(0)
     table[b, 24:32, :] = jnp.zeros((8, LO), F32)
     table[b, 56:64, :] = jnp.zeros((8, LO), F32)
     for r in range(HALF_ROWS):
-        lanes = slice(r * LO, (r + 1) * LO)
-        table[b, r : r + 1, :] = fdisp[0:1, lanes]
-        table[b, PAD_ROWS + r : PAD_ROWS + r + 1, :] = fdisp[1:2, lanes]
-    pl.semaphore_wait(barrier, 5)
-
-    send(table.at[b], table.at[b], 0, 0, (d, o))
+        for c in range(2):
+            at = PAD_ROWS * c + r
+            table[b, at : at + 1, :] = fdisp[c : c + 1, r * LO : (r + 1) * LO]
+    pl.semaphore_wait(
+        barrier, 1 + 2 * has_left.astype(I32) + 2 * has_right.astype(I32)
+    )
+
+    send(table.at[b], table.at[b], 0, 0, (d, o), None)
     slots = (own, 8 + 2 * b, 8 + 2 * b, 2 * b, 2 * b)
     marks = (0, 3 + b, 3 + b, 1 + b, 1 + b)
     for j in range(5):
@@ -157,22 +233,29 @@
             3 + j,
             3 + marks[j],
             peers[j],
-        )
-    send(pmat.at[0], pm.at[b], 1, 1, (d, o))
+            there[j],
+        )
+    loaded(5)
+    send(pm.at[b], pm.at[b], 1, 1, (d, o), None)
     sources = (theirs, 0, 2, 8, 10)
 
     speed[b, 24:32, :] = jnp.zeros((8, LO), F32)
     speed[b, 56:64, :] = jnp.zeros((8, LO), F32)
     speed[b, 88:96, :] = jnp.zeros((8, LO), F32)
+    loaded(6, 7)
     for r in range(HALF_ROWS):
-        lanes = slice(r * LO, (r + 1) * LO)
-        speed[b, r : r + 1, :] = fvel[0:1, lanes]
-        speed[b, PAD_ROWS + r : PAD_ROWS + r + 1, :] = fvel[1:2, lanes]
-        speed[b, 2 * PAD_ROWS + r : 2 * PAD_ROWS + r + 1, :] = fstep[0:1, lanes]
-    send(speed.at[b], speed.at[b], 2, 2, (d, o))
-    pm[b] = pmat[0]
-    states = (started[0], started.pop())
+        for c in range(2):
+            at = PAD_ROWS * c + r
+            speed[b, at : at + 1, :] = fvel[c : c + 1, r * LO : (r + 1) * LO]
+    for p in range(2):
+        lanes = slice(p * 128, (p + 1) * 128)
+        speed[b, 2 * PAD_ROWS : 2 * PAD_ROWS + HALF_ROWS, lanes] = fstep[
+            pl.ds(p, HALF_ROWS, stride=2), :
+        ]
+    send(speed.at[b], speed.at[b], 2, 2, (d, o), None)
+    states = (started[0][0], started.pop()[0])
     del started[0]
+    loaded(*range(8, 20))
 
     lo_iota = lax.broadcasted_iota(I32, (LO, 128), 0)
 
@@ -206,7 +289,7 @@
     scale = weight * fmod[...]
 
     for j in range(5):
-        arrived(pdx.at[pl.ds(sources[j], 2)], 3 + j)
+        arrived(pdx.at[pl.ds(sources[j], 2)], 3 + j, there[j])
 
     ids[...] = jnp.full((8, 128), -1, I32)
     ids[pl.ds(b, 1), :] = pnodes[...]
@@ -272,8 +355,8 @@
         ub, st = (ub0, ub1)[s], (st0, st1)[s]
         base = 8 + 13 * s
         if s == 0:
-            arrived(table.at[o], 0)
-            arrived(pm.at[o], 1)
+            arrived(table.at[o], 0, None)
+            arrived(pm.at[o], 1, None)
 
         top, low = split2(table[...].reshape(128, LO))
         split_table[0:128, :] = top
@@ -302,8 +385,8 @@
                     hit, u + pblend[q : q + 1, :] * (targets[q] - u), new
                 )
             ub[4 + k] = new
-        send(ub.at[pl.ds(4, 4)], ub.at[pl.ds(8, 4)], base, base + 1, (left, b))
-        send(ub.at[pl.ds(4, 4)], ub.at[pl.ds(0, 4)], base + 1, base, (right, b))
+        send(ub.at[pl.ds(4, 4)], ub.at[pl.ds(8, 4)], base, base + 1, (left, b), has_left)
+        send(ub.at[pl.ds(4, 4)], ub.at[pl.ds(0, 4)], base + 1, base, (right, b), has_right)
 
         @pl.loop(0, 64 // CHUNK)
         def _(i):
@@ -322,8 +405,8 @@
                     [f[c] for f in found], axis=0
                 )
 
-        arrived(ub.at[pl.ds(0, 4)], base)
-        arrived(ub.at[pl.ds(8, 4)], base + 1)
+        arrived(ub.at[pl.ds(0, 4)], base, has_left)
+        arrived(ub.at[pl.ds(8, 4)], base + 1, has_right)
 
         @pl.loop(0, 6)
         def _(p):
@@ -366,6 +449,7 @@
                 base + 2 + j,
                 base + 2 + marks[j],
                 peers[j],
+                there[j],
             )
 
         grad = jnp.dot(sgrad[...], del_[...], precision=EXACT, preferred_element_type=F32)
@@ -413,11 +497,16 @@
         partial = acc[0:128, :] + acc[128:256, :]
         pel_send[s] = partial
         if s == 0:
-            send(pel_send.at[s], pel_recv.at[s], base + 7, base + 7, (d, o))
+            send(pel_send.at[s], pel_recv.at[s], base + 7, base + 7, (d, o), None)
         else:
             cut = pl.ds(o * 64, 64)
             send(
-                pel_send.at[s, cut], pel_recv.at[s, cut], base + 7, base + 7, (d, o)
+                pel_send.at[s, cut],
+                pel_recv.at[s, cut],
+                base + 7,
+                base + 7,
+                (d, o),
+                None,
             )
         top, low = split2(partial)
         product = jnp.dot(
@@ -434,7 +523,7 @@
             border.append(jnp.concatenate(found, axis=0))
 
         for j in range(5):
-            arrived(st.at[pl.ds(sources[j], 2)], base + 2 + j)
+            arrived(st.at[pl.ds(sources[j], 2)], base + 2 + j, there[j])
 
         def coefficients(k, state):
             theta, volume = state[0:1, :], state[1:2, :]
@@ -483,7 +572,7 @@
             )
         late = jnp.concatenate(reaction + moved, axis=0)
         late_send[s] = late
-        send(late_send.at[s], late_recv.at[s], base + 8, base + 8, (d, o))
+        send(late_send.at[s], late_recv.at[s], base + 8, base + 8, (d, o), None)
         wide = jnp.concatenate(reaction, axis=1)
         top, low = split2(wide)
         met = jnp.dot(
@@ -502,6 +591,7 @@
                 base + 9 + j,
                 base + 9 + 2 * (1 - side) + b,
                 peers[1 + j],
+                there[1 + j],
             )
         if s == 0:
             for t in range(2):
@@ -511,13 +601,13 @@
                 disp_out[t] = moved[t]
                 vel_out[t] = cur[t]
 
-        arrived(late_recv.at[s], base + 8)
+        arrived(late_recv.at[s], base + 8, None)
         other = late_recv[s]
         if s == 0:
             for t in range(2):
                 ub1[theirs + t] = other[4 + 2 * t : 6 + 2 * t, :]
         for j in range(4):
-            arrived(bd_recv.at[s, j], base + 9 + j)
+            arrived(bd_recv.at[s, j], base + 9 + j, there[1 + j])
         shared = [
             jnp.where(
                 jnp.full((2, 128), d, I32) > 0, bd_recv[s, 0] + bd_recv[s, 1], 0.0
@@ -543,12 +633,12 @@
         extra = nt(jnp.concatenate(sides, axis=1), onehot[:, 8192:8704])
         acc[0:128, :] = extra[0:128, :] + extra[128:256, :]
         if s == 0:
-            arrived(speed.at[o], 2)
-            arrived(pel_recv.at[s], base + 7)
+            arrived(speed.at[o], 2, None)
+            arrived(pel_recv.at[s], base + 7, None)
             for copy in states:
                 copy.wait_send()
         else:
-            arrived(pel_recv.at[s, pl.ds(b * 64, 64)], base + 7)
+            arrived(pel_recv.at[s, pl.ds(b * 64, 64)], base + 7, None)
         for h in range(2) if s == 0 else (b,):
             for c in range(2):
                 cut = pl.ds(h * 64 + c * 32, 32)
@@ -564,8 +654,20 @@
             at = PAD_ROWS * c + r
             fdisp_out[c : c + 1, lanes] = table[b, at : at + 1, :]
             fvel_out[c : c + 1, lanes] = speed[b, at : at + 1, :]
-    for copy in started:
-        copy.wait_send()
+    for copy, cond in started:
+        if_there(cond, copy.wait_send)
+
+
+def hand_over(*refs):
+    ins, outs, sems = refs[:4], refs[4:8], refs[8]
+    copies = [
+        pltpu.make_async_copy(src, dst, sems.at[at])
+        for at, (src, dst) in enumerate(zip(ins, outs))
+    ]
+    for copy in copies:
+        copy.start()
+    for copy in copies:
+        copy.wait()
 
 
 def shards(n_dom, *args):
@@ -592,15 +694,13 @@
         shared_right,
     ) = args
     vmem = pl.BlockSpec(memory_space=pltpu.VMEM)
-    smem = pl.BlockSpec(memory_space=pltpu.SMEM)
-    in_specs = [vmem] * 20
-    for at in (5, 6, 7):
-        in_specs[at] = smem
+    hbm = pl.BlockSpec(memory_space=pltpu.HBM)
+    rows = fe_step.shape[0] // 128
 
     def f32(*shape):
         return pltpu.VMEM(shape, F32)
 
-    return pl.pallas_call(
+    results = pl.pallas_call(
         functools.partial(kernel, n_dom),
         out_shape=[
             jax.ShapeDtypeStruct(pd_disp.shape, F32),
@@ -608,9 +708,28 @@
             jax.ShapeDtypeStruct(fe_disp.shape, F32),
             jax.ShapeDtypeStruct(fe_vel.shape, F32),
         ],
-        in_specs=in_specs,
+        in_specs=[hbm] * 20,
         out_specs=[vmem] * 4,
         scratch_shapes=[
+            f32(2, 2, 128),
+            f32(2, 2, 128),
+            f32(2, 2, 128),
+            f32(2, 128),
+            f32(2, 128),
+            pltpu.SMEM((2, 3), I32),
+            pltpu.SMEM((1,), I32),
+            pltpu.SMEM((2,), I32),
+            f32(2, 128),
+            pltpu.VMEM((1, 128), I32),
+            f32(*fe_disp.shape),
+            f32(*fe_vel.shape),
+            f32(rows, 128),
+            f32(1, 128),
+            pltpu.VMEM((64, 128), I32),
+            f32(128, 64),
+            f32(1, 64),
+            pltpu.VMEM((1, 113), I32),
+            pltpu.VMEM((1, 113), I32),
             f32(12, 8, 128),
             f32(12, 2, 128),
             f32(12, 2, 128),
@@ -639,9 +758,10 @@
             f32(2, 4, 2, 128),
             pltpu.SemaphoreType.DMA((N_COPIES,)),
             pltpu.SemaphoreType.DMA((N_COPIES,)),
+            pltpu.SemaphoreType.DMA((20,)),
         ],
         compiler_params=pltpu.CompilerParams(
-            collective_id=0, has_side_effects=True, vmem_limit_bytes=40 * 2**20
+            collective_id=0, has_side_effects=True, vmem_limit_bytes=VMEM_BYTES
         ),
     )(
         pd_disp,
@@ -657,7 +777,7 @@
         patch_matrix,
         fe_disp,
         fe_vel,
-        fe_step.reshape(1, -1),
+        fe_step.reshape(-1, 128),
         fe_modulus.reshape(1, -1),
         element_nodes,
         shape_grad.reshape(-1, shape_grad.shape[2]),
@@ -665,6 +785,14 @@
         shared_left,
         shared_right,
     )
+    return pl.pallas_call(
+        hand_over,
+        out_shape=[jax.ShapeDtypeStruct(x.shape, F32) for x in results],
+        in_specs=[hbm] * 4,
+        out_specs=[hbm] * 4,
+        scratch_shapes=[pltpu.SemaphoreType.DMA((4,))],
+        compiler_params=pltpu.CompilerParams(vmem_limit_bytes=VMEM_BYTES),
+    )(*results)
 
 
 def solution(mesh):

time: 74.6 us -> 59.6 us (0.80)
  the two profiles are of different devices: /device:TPU:1 before, /device:TPU:257 now
where the time goes in v2:
time: 59.6 us; the launch traced here: 59.4 us
  Pallas kernels  58.1 us (97%)
  between operations  1.29 us (2%)
    pallas_call x1, Pallas kernels, shards(): pl.pallas_call(functools.partial(kernel, n_dom), out_shape=[jax.ShapeDtyp...  53.8 us
    pallas_call x1, Pallas kernels, shards(): pl.pallas_call(hand_over, out_shape=[jax.ShapeDtypeStruct(x.shape, F32) f...  4.37 us

profile of v2, /device:TPU:257, one launch (start us, length us, event | category | flops | bytes accessed | tf_op | source)
XLA Modules:
  0.0 59.4 jit_solution(8916608161745878234)
XLA Ops:
  1.3 53.8 %shard_map.219 = (f32[2,2,128]{2,1,0:T(2,128)}, f32[2,2,128]{2,1,0:T(2,128)}, f32[2,6400]{1,0:T(2,128)}, f32[2,6400]{1,0:T(2,128)}) custom-call(f32[2,2,128]{2,1,0:T(2,128)} %disp_in.1, f32[2,2,128]{2,1,0:T(2,128)} %vel_in.1, f32[2,2,128]{2,1,0:T(2,128)} %coord_in.1, f32[2,128]{1,0:T(2,128)} %modulus_in.1, f32[2,128]{1,0:T(2,128)} %step_in.1, ...), custom_call_target="tpu_custom_call" | custom-call | tf_op jit(solution)/shard_map/pallas_call | solution.py:703
  55.1 4.4 %shard_map.220 = (f32[2,2,128]{2,1,0:T(2,128)}, f32[2,2,128]{2,1,0:T(2,128)}, f32[2,6400]{1,0:T(2,128)}, f32[2,6400]{1,0:T(2,128)}) custom-call(f32[2,2,128]{2,1,0:T(2,128)} %get-tuple-element.8.refs_0_, f32[2,2,128]{2,1,0:T(2,128)} %get-tuple-element.9.refs_1_, f32[2,6400]{1,0:T(2,128)} %get-tuple-element.10.refs_2_, f32[2,6400]{1,0:T(2,128)} %get-tuple-element.11.refs_3_), custom_call_target="tpu_custom_call" | custom-call | tf_op jit(solution)/shard_map/pallas_call | solution.py:788

commit v3 on v2

--- a/solution.py
+++ b/solution.py
@@ -28,6 +28,15 @@
 def split2(x):
     top = x.astype(BF16)
     return top, (x - top.astype(F32)).astype(BF16)
+
+
+def folded(x):
+    return jnp.sum(x.reshape(-1, 8, x.shape[1]), axis=0)
+
+
+def inverted(x):
+    y = pl.reciprocal(x, approx=True)
+    return y * (2.0 - x * y)
 
 
 def nt(a, b, **kw):
@@ -99,7 +108,6 @@
     sgt,
     acc,
     bonds,
-    sums,
     cur,
     pel_send,
     pel_recv,
@@ -219,6 +227,61 @@
         for c in range(2):
             at = PAD_ROWS * c + r
             table[b, at : at + 1, :] = fdisp[c : c + 1, r * LO : (r + 1) * LO]
+    loaded(6, 7)
+    speed[b, 24:32, :] = jnp.zeros((8, LO), F32)
+    speed[b, 56:64, :] = jnp.zeros((8, LO), F32)
+    speed[b, 88:96, :] = jnp.zeros((8, LO), F32)
+    for r in range(HALF_ROWS):
+        for c in range(2):
+            at = PAD_ROWS * c + r
+            speed[b, at : at + 1, :] = fvel[c : c + 1, r * LO : (r + 1) * LO]
+    for p in range(2):
+        lanes = slice(p * 128, (p + 1) * 128)
+        speed[b, 2 * PAD_ROWS : 2 * PAD_ROWS + HALF_ROWS, lanes] = fstep[
+            pl.ds(p, HALF_ROWS, stride=2), :
+        ]
+    loaded(*range(8, 20))
+
+    lo_iota = lax.broadcasted_iota(I32, (LO, 128), 0)
+
+    def table_row(node):
+        hi = lax.shift_right_arithmetic(node, 8)
+        return jnp.where(hi >= HALF_ROWS, hi + (PAD_ROWS - HALF_ROWS), hi)
+
+    def onehot_of(lo_row):
+        return jnp.where(
+            lo_iota == jnp.broadcast_to(lo_row, (LO, 128)), 1.0, 0.0
+        ).astype(BF16)
+
+    @pl.loop(0, 64 // CHUNK)
+    def _(i):
+        node = enodes[pl.ds(pl.multiple_of(i * CHUNK, CHUNK), CHUNK), :]
+        hrow[pl.ds(pl.multiple_of(i * CHUNK, CHUNK), CHUNK), :] = table_row(node)
+        lo = lax.bitwise_and(node, LO - 1)
+        base = pl.multiple_of(i * (CHUNK * 128), CHUNK * 128)
+        for g in range(CHUNK):
+            onehot[:, pl.ds(base + g * 128, 128)] = onehot_of(lo[g : g + 1, :])
+
+    sgt[...] = sgrad[...].T
+    eye = lax.broadcasted_iota(I32, (64, 64), 0) == lax.broadcasted_iota(
+        I32, (64, 64), 1
+    )
+    weight = jnp.sum(
+        jnp.where(eye, jnp.broadcast_to(qweight[...], (64, 64)), 0.0),
+        axis=1,
+        keepdims=True,
+    )
+    scale = weight * fmod[...]
+
+
+    ids[...] = jnp.full((8, 128), -1, I32)
+    ids[pl.ds(b, 1), :] = pnodes[...]
+    ids[2:3, 0:113] = sleft[...]
+    ids[3:4, 0:113] = sright[...]
+    few_lo = lax.bitwise_and(ids[...], LO - 1)
+    for g in (2, 3):
+        onehot[:, 8192 + g * 128 : 8320 + g * 128] = onehot_of(few_lo[g : g + 1, :])
+
     pl.semaphore_wait(
         barrier, 1 + 2 * has_left.astype(I32) + 2 * has_right.astype(I32)
     )
@@ -238,94 +301,39 @@
     loaded(5)
     send(pm.at[b], pm.at[b], 1, 1, (d, o), None)
     sources = (theirs, 0, 2, 8, 10)
-
-    speed[b, 24:32, :] = jnp.zeros((8, LO), F32)
-    speed[b, 56:64, :] = jnp.zeros((8, LO), F32)
-    speed[b, 88:96, :] = jnp.zeros((8, LO), F32)
-    loaded(6, 7)
-    for r in range(HALF_ROWS):
-        for c in range(2):
-            at = PAD_ROWS * c + r
-            speed[b, at : at + 1, :] = fvel[c : c + 1, r * LO : (r + 1) * LO]
-    for p in range(2):
-        lanes = slice(p * 128, (p + 1) * 128)
-        speed[b, 2 * PAD_ROWS : 2 * PAD_ROWS + HALF_ROWS, lanes] = fstep[
-            pl.ds(p, HALF_ROWS, stride=2), :
-        ]
     send(speed.at[b], speed.at[b], 2, 2, (d, o), None)
     states = (started[0][0], started.pop()[0])
     del started[0]
-    loaded(*range(8, 20))
-
-    lo_iota = lax.broadcasted_iota(I32, (LO, 128), 0)
-
-    def table_row(node):
-        hi = lax.shift_right_arithmetic(node, 8)
-        return jnp.where(hi >= HALF_ROWS, hi + (PAD_ROWS - HALF_ROWS), hi)
-
-    def onehot_of(lo_row):
-        return jnp.where(
-            lo_iota == jnp.broadcast_to(lo_row, (LO, 128)), 1.0, 0.0
-        ).astype(BF16)
-
-    @pl.loop(0, 64 // CHUNK)
-    def _(i):
-        node = enodes[pl.ds(pl.multiple_of(i * CHUNK, CHUNK), CHUNK), :]
-        hrow[pl.ds(pl.multiple_of(i * CHUNK, CHUNK), CHUNK), :] = table_row(node)
-        lo = lax.bitwise_and(node, LO - 1)
-        base = pl.multiple_of(i * (CHUNK * 128), CHUNK * 128)
-        for g in range(CHUNK):
-            onehot[:, pl.ds(base + g * 128, 128)] = onehot_of(lo[g : g + 1, :])
-
-    sgt[...] = sgrad[...].T
-    eye = lax.broadcasted_iota(I32, (64, 64), 0) == lax.broadcasted_iota(
-        I32, (64, 64), 1
-    )
-    weight = jnp.sum(
-        jnp.where(eye, jnp.broadcast_to(qweight[...], (64, 64)), 0.0),
-        axis=1,
-        keepdims=True,
-    )
-    scale = weight * fmod[...]
-
-    for j in range(5):
-        arrived(pdx.at[pl.ds(sources[j], 2)], 3 + j, there[j])
-
-    ids[...] = jnp.full((8, 128), -1, I32)
-    ids[pl.ds(b, 1), :] = pnodes[...]
+
+    arrived(pdx.at[pl.ds(theirs, 2)], 3, None)
     ids[pl.ds(o, 1), :] = pdx[theirs, 5:6, :].astype(I32)
-    ids[2:3, 0:113] = sleft[...]
-    ids[3:4, 0:113] = sright[...]
     few = ids[...]
     hrow[64:72, :] = table_row(few)
     few_lo = lax.bitwise_and(few, LO - 1)
-    for g in range(4):
+    for g in range(2):
         onehot[:, 8192 + g * 128 : 8320 + g * 128] = onehot_of(few_lo[g : g + 1, :])
-    few_f = few.astype(F32)
-    few_t = few_f.T
-    for q in range(2):
-        for side in range(2):
-            link[q * 128 : (q + 1) * 128, side * 128 : (side + 1) * 128] = jnp.where(
-                few_t[:, q : q + 1] == few_f[2 + side : 3 + side, :], 1.0, 0.0
-            ).astype(BF16)
 
     OX, OY, REST, INFL0, NX, NY, STR, INFL = range(8)
-
-    @pl.loop(0, 6)
-    def _(p):
-        t = p // 3
-        far = pdx[family[t, p - 3 * t]]
-        far_t = far.T
-        me = pdx[own + t]
-        ox = far_t[:, 0:1] - me[0:1, :]
-        oy = far_t[:, 1:2] - me[1:2, :]
-        r2 = ox * ox + oy * oy
-        bonds[OX, p] = ox
-        bonds[OY, p] = oy
-        bonds[REST, p] = jnp.sqrt(r2 + CORE_SQ)
-        bonds[INFL0, p] = jnp.exp(-0.5 * r2)
-
     cur[...] = vel[...]
+
+    def pair(p):
+        return p // 3, p % 3
+
+    def keep_bonds():
+        for p in range(6):
+            t, k = pair(p)
+            far_t = pdx[family[t, k]].T
+            me = pdx[own + t]
+            for q in range(0, 128, 32):
+                rows = slice(q, q + 32)
+                ox = far_t[rows, 0:1] - me[0:1, :]
+                oy = far_t[rows, 1:2] - me[1:2, :]
+                r2 = ox * ox + oy * oy
+                bonds[OX, p, rows] = ox
+                bonds[OY, p, rows] = oy
+                bonds[REST, p, rows] = jnp.sqrt(r2 + CORE_SQ)
+                bonds[INFL0, p, rows] = jnp.exp(-0.5 * r2)
+
     row_iota = lax.broadcasted_iota(I32, (64, 128), 0)
 
     def masked_rows(product, row):
@@ -405,43 +413,53 @@
                     [f[c] for f in found], axis=0
                 )
 
+        if s == 0:
+            few_f = ids[...].astype(F32)
+            few_t = few_f.T
+            for q in range(2):
+                for side in range(2):
+                    link[
+                        q * 128 : (q + 1) * 128, side * 128 : (side + 1) * 128
+                    ] = jnp.where(
+                        few_t[:, q : q + 1] == few_f[2 + side : 3 + side, :], 1.0, 0.0
+                    ).astype(BF16)
+
+        if s == 0:
+            for j in range(1, 5):
+                arrived(pdx.at[pl.ds(sources[j], 2)], 3 + j, there[j])
+            keep_bonds()
+
         arrived(ub.at[pl.ds(0, 4)], base, has_left)
         arrived(ub.at[pl.ds(8, 4)], base + 1, has_right)
 
-        @pl.loop(0, 6)
-        def _(p):
-            t = p // 3
-            far = ub[family[t, p - 3 * t]]
-            far_t = jnp.concatenate([far, jnp.zeros((6, 128), F32)], axis=0).T
+        totals = [[jnp.zeros((8, 128), F32)] * 2 for _ in range(2)]
+        for p in range(6):
+            t, k = pair(p)
+            far_t = jnp.concatenate([ub[family[t, k]], jnp.zeros((6, 128), F32)], axis=0).T
             me = ub[own + t]
-            yx = bonds[OX, p] + (far_t[:, 0:1] - me[0:1, :])
-            yy = bonds[OY, p] + (far_t[:, 1:2] - me[1:2, :])
-            y2 = yx * yx + yy * yy + CORE_SQ
-            length = jnp.sqrt(y2)
-            inverse = 1.0 / length
-            rest = bonds[REST, p]
-            stretch = length - rest
-            ratio = stretch * (1.0 / STRETCH)
-            influence = bonds[INFL0, p] / (1.0 + ratio * ratio)
-            bonds[NX, p] = yx * inverse
-            bonds[NY, p] = yy * inverse
-            bonds[STR, p] = stretch
-            bonds[INFL, p] = influence
-            weighted = influence * rest
-            sums[p] = jnp.concatenate(
-                [
-                    jnp.sum(weighted * stretch, axis=0, keepdims=True),
-                    jnp.sum(weighted * rest, axis=0, keepdims=True),
-                ],
-                axis=0,
-            )
+            for q in range(0, 128, 32):
+                rows = slice(q, q + 32)
+                yx = bonds[OX, p, rows] + (far_t[rows, 0:1] - me[0:1, :])
+                yy = bonds[OY, p, rows] + (far_t[rows, 1:2] - me[1:2, :])
+                y2 = yx * yx + yy * yy + CORE_SQ
+                inverse = lax.rsqrt(y2)
+                length = y2 * inverse
+                rest = bonds[REST, p, rows]
+                stretch = length - rest
+                ratio = stretch * (1.0 / STRETCH)
+                influence = bonds[INFL0, p, rows] * inverted(1.0 + ratio * ratio)
+                bonds[NX, p, rows] = yx * inverse
+                bonds[NY, p, rows] = yy * inverse
+                bonds[STR, p, rows] = stretch
+                bonds[INFL, p, rows] = influence
+                weighted = influence * rest
+                totals[t][0] = totals[t][0] + folded(weighted * stretch)
+                totals[t][1] = totals[t][1] + folded(weighted * rest)
+        totals = [[jnp.sum(x, axis=0, keepdims=True) for x in y] for y in totals]
 
         for t in range(2):
-            total = sums[3 * t] + sums[3 * t + 1] + sums[3 * t + 2]
-            volume = total[1:2, :]
-            st[own + t] = jnp.concatenate(
-                [2.0 * total[0:1, :] / volume, volume], axis=0
-            )
+            dilated, volume = totals[t]
+            st[own + t] = jnp.concatenate([2.0 * dilated / volume, volume], axis=0)
         for j in range(5):
             send(
                 st.at[pl.ds(own, 2)],
@@ -529,31 +547,31 @@
             theta, volume = state[0:1, :], state[1:2, :]
             return 2.0 * k * theta / volume, 4.0 * k / volume, 0.5 * theta
 
-        @pl.loop(0, 6)
-        def _(p):
-            t = p // 3
-            j = family[t, p - 3 * t]
-            fa, fb, fc = coefficients(pdx[j][2:3, :], st[j])
-            far_t = jnp.concatenate([fa, fb, fc, jnp.zeros((5, 128), F32)], axis=0).T
-            oa, ob, oc = coefficients(pdx[own + t][2:3, :], st[own + t])
-            rest = bonds[REST, p]
-            stretch = bonds[STR, p]
-            near = oa * rest + ob * (stretch - oc * rest)
-            away = far_t[:, 0:1] * rest + far_t[:, 1:2] * (stretch - far_t[:, 2:3] * rest)
-            force = bonds[INFL, p] * (near + away)
-            sums[p] = jnp.concatenate(
-                [
-                    jnp.sum(force * bonds[NX, p], axis=0, keepdims=True),
-                    jnp.sum(force * bonds[NY, p], axis=0, keepdims=True),
-                ],
-                axis=0,
-            )
+        totals = [[jnp.zeros((8, 128), F32)] * 2 for _ in range(2)]
+        near = [coefficients(pdx[own + t][2:3, :], st[own + t]) for t in range(2)]
+        for p in range(6):
+            t, k = pair(p)
+            j = family[t, k]
+            far = coefficients(pdx[j][2:3, :], st[j])
+            far_t = jnp.concatenate(far + (jnp.zeros((5, 128), F32),), axis=0).T
+            oa, ob, oc = near[t]
+            for q in range(0, 128, 32):
+                rows = slice(q, q + 32)
+                rest = bonds[REST, p, rows]
+                stretch = bonds[STR, p, rows]
+                mine = oa * rest + ob * (stretch - oc * rest)
+                away = far_t[rows, 0:1] * rest + far_t[rows, 1:2] * (
+                    stretch - far_t[rows, 2:3] * rest
+                )
+                force = bonds[INFL, p, rows] * (mine + away)
+                totals[t][0] = totals[t][0] + folded(force * bonds[NX, p, rows])
+                totals[t][1] = totals[t][1] + folded(force * bonds[NY, p, rows])
 
         forces, moved = [], []
         for t in range(2):
             alive = jnp.full((2, 128), 2 * b + t, I32) < live[0]
-            total = sums[3 * t] + sums[3 * t + 1] + sums[3 * t + 2]
-            force = jnp.where(alive, total, 0.0)
+            total = [jnp.sum(x, axis=0, keepdims=True) for x in totals[t]]
+            force = jnp.where(alive, jnp.concatenate(total, axis=0), 0.0)
             forces.append(force)
             v = jnp.where(alive, cur[t] + step[t : t + 1, :] * force, 0.0)
             u = jnp.where(alive, ub[own + t] + TIME_STEP * v, 0.0)
@@ -703,10 +721,10 @@
     results = pl.pallas_call(
         functools.partial(kernel, n_dom),
         out_shape=[
-            jax.ShapeDtypeStruct(pd_disp.shape, F32),
-            jax.ShapeDtypeStruct(pd_vel.shape, F32),
-            jax.ShapeDtypeStruct(fe_disp.shape, F32),
-            jax.ShapeDtypeStruct(fe_vel.shape, F32),
+            pltpu.VMEM(pd_disp.shape, F32),
+            pltpu.VMEM(pd_vel.shape, F32),
+            pltpu.VMEM(fe_disp.shape, F32),
+            pltpu.VMEM(fe_vel.shape, F32),
         ],
         in_specs=[hbm] * 20,
         out_specs=[vmem] * 4,
@@ -748,7 +766,6 @@
             f32(64, 128),
             f32(256, LO),
             f32(8, 6, 128, 128),
-            f32(6, 2, 128),
             f32(2, 2, 128),
             f32(2, 128, LO),
             f32(2, 128, LO),
@@ -788,10 +805,10 @@
     return pl.pallas_call(
         hand_over,
         out_shape=[jax.ShapeDtypeStruct(x.shape, F32) for x in results],
-        in_specs=[hbm] * 4,
+        in_specs=[vmem] * 4,
         out_specs=[hbm] * 4,
         scratch_shapes=[pltpu.SemaphoreType.DMA((4,))],
-        compiler_params=pltpu.CompilerParams(vmem_limit_bytes=VMEM_BYTES),
+        compiler_params=pltpu.CompilerParams(vmem_limit_bytes=2**20),
     )(*results)
 
 

time: 59.6 us -> 46.5 us (0.78)
  Pallas kernels: 58.1 us -> 45.1 us
    pallas_call x1, Pallas kernels: 53.8 us -> 44.4 us  [shards(): pl.pallas_call(functools.partial(kernel, n_dom), out_shape=[pltpu.VMEM(pd...]
    pallas_call x1, Pallas kernels: 4.37 us -> 0.68 us  [shards(): pl.pallas_call(hand_over, out_shape=[jax.ShapeDtypeStruct(x.shape, F32) f...]
where the time goes in v3:
time: 46.5 us; the launch traced here: 46.3 us
  Pallas kernels  45.1 us (97%)
  between operations  1.29 us (3%)
    pallas_call x1, Pallas kernels, shards(): pl.pallas_call(functools.partial(kernel, n_dom), out_shape=[pltpu.VMEM(pd...  44.4 us

profile of v3, /device:TPU:257, one launch (start us, length us, event | category | flops | bytes accessed | tf_op | source)
XLA Modules:
  0.0 46.3 jit_solution(3859951489875712674)
XLA Ops:
  1.3 44.4 %shard_map.219 = (f32[2,2,128]{2,1,0:T(2,128)S(1)}, f32[2,2,128]{2,1,0:T(2,128)S(1)}, f32[2,6400]{1,0:T(2,128)S(1)}, f32[2,6400]{1,0:T(2,128)S(1)}) custom-call(f32[2,2,128]{2,1,0:T(2,128)} %disp_in.1, f32[2,2,128]{2,1,0:T(2,128)} %vel_in.1, f32[2,2,128]{2,1,0:T(2,128)} %coord_in.1, f32[2,128]{1,0:T(2,128)} %modulus_in.1, f32[2,128]{1,0:T(2,128)} %step_in.1, ...), custom_call_target="tpu_custom_call" | custom-call | tf_op jit(solution)/shard_map/pallas_call | solution.py:721
  45.7 0.7 %shard_map.220 = (f32[2,2,128]{2,1,0:T(2,128)}, f32[2,2,128]{2,1,0:T(2,128)}, f32[2,6400]{1,0:T(2,128)}, f32[2,6400]{1,0:T(2,128)}) custom-call(f32[2,2,128]{2,1,0:T(2,128)S(1)} %get-tuple-element.8.refs_0_, f32[2,2,128]{2,1,0:T(2,128)S(1)} %get-tuple-element.9.refs_1_, f32[2,6400]{1,0:T(2,128)S(1)} %get-tuple-element.10.refs_2_, ...), custom_call_target="tpu_custom_call" | custom-call | tf_op jit(solution)/shard_map/pallas_call | solution.py:805

commit v4 on v3

--- a/solution.py
+++ b/solution.py
@@ -21,7 +21,7 @@
 HALF_ROWS = 25
 PAD_ROWS = 32
 CHUNK = 8
-N_COPIES = 34
+N_COPIES = 37
 VMEM_BYTES = 60 * 2**20
 
 
@@ -93,8 +93,9 @@
     pdx,
     ub0,
     ub1,
-    st0,
-    st1,
+    lists_in,
+    lists_sent,
+    lists,
     pm,
     table,
     speed,
@@ -108,6 +109,8 @@
     sgt,
     acc,
     bonds,
+    far_bonds,
+    far_state,
     cur,
     pel_send,
     pel_recv,
@@ -124,10 +127,18 @@
     o = 1 - b
     has_left = d > 0
     has_right = d < n_dom - 1
+    has_left2 = d > 1
+    has_right2 = d < n_dom - 2
     left = jnp.maximum(d - 1, 0)
     right = jnp.minimum(d + 1, n_dom - 1)
-    peers = ((d, o), (left, 0), (left, 1), (right, 0), (right, 1))
-    there = (None, has_left, has_left, has_right, has_right)
+    left2 = jnp.maximum(d - 2, 0)
+    right2 = jnp.minimum(d + 2, n_dom - 1)
+    peers = ((d, o),) + tuple(
+        (x, j) for x in (left, right, left2, right2) for j in range(2)
+    )
+    there = (None,) + tuple(
+        x for x in (has_left, has_right, has_left2, has_right2) for j in range(2)
+    )
 
     def if_there(cond, act):
         if cond is None:
@@ -163,6 +174,7 @@
             (vel_in, vel),
             (step_in, step),
             (family_in, family),
+            (family_in, lists_in),
             (live_in, live),
             (ptile_in, ptile),
             (pblend_in, pblend),
@@ -205,8 +217,8 @@
         )
         if_there(cond, copy.wait_recv)
 
-    own = 4 + 2 * b
-    theirs = 4 + 2 * o
+    own = 8 + 2 * b
+    theirs = 8 + 2 * o
 
     loaded(1, 2, 3, 4)
     for t in range(2):
@@ -240,7 +252,7 @@
         speed[b, 2 * PAD_ROWS : 2 * PAD_ROWS + HALF_ROWS, lanes] = fstep[
             pl.ds(p, HALF_ROWS, stride=2), :
         ]
-    loaded(*range(8, 20))
+    loaded(*range(8, 21))
 
     lo_iota = lax.broadcasted_iota(I32, (LO, 128), 0)
 
@@ -274,6 +286,17 @@
     scale = weight * fmod[...]
 
 
+    lists_sent[2 + b] = jnp.zeros((8, 128), I32)
+    lists_sent[2 + b, 0:2, 0:3] = lists_in[...]
+
+    @pl.when(jnp.logical_not(has_left))
+    def _():
+        lists_sent[0:2] = jnp.zeros((2, 8, 128), I32)
+
+    @pl.when(jnp.logical_not(has_right))
+    def _():
+        lists_sent[4:6] = jnp.zeros((2, 8, 128), I32)
+
     ids[...] = jnp.full((8, 128), -1, I32)
     ids[pl.ds(b, 1), :] = pnodes[...]
     ids[2:3, 0:113] = sleft[...]
@@ -283,13 +306,16 @@
         onehot[:, 8192 + g * 128 : 8320 + g * 128] = onehot_of(few_lo[g : g + 1, :])
 
     pl.semaphore_wait(
-        barrier, 1 + 2 * has_left.astype(I32) + 2 * has_right.astype(I32)
+        barrier, 1 + 2 * sum(x.astype(I32) for x in (has_left, has_right, has_left2, has_right2))
     )
 
     send(table.at[b], table.at[b], 0, 0, (d, o), None)
-    slots = (own, 8 + 2 * b, 8 + 2 * b, 2 * b, 2 * b)
-    marks = (0, 3 + b, 3 + b, 1 + b, 1 + b)
-    for j in range(5):
+    slots = (own,) + tuple(x + 2 * b for x in (12, 12, 4, 4, 16, 16, 0, 0))
+    marks = (0,) + tuple(x + b for x in (3, 3, 1, 1, 7, 7, 5, 5))
+    homes = (2 + b,) + tuple(x + b for x in (4, 4, 0, 0))
+    loaded(5)
+    send(pm.at[b], pm.at[b], 1, 1, (d, o), None)
+    for j in range(9):
         send(
             pdx.at[pl.ds(own, 2)],
             pdx.at[pl.ds(slots[j], 2)],
@@ -298,12 +324,20 @@
             peers[j],
             there[j],
         )
-    loaded(5)
-    send(pm.at[b], pm.at[b], 1, 1, (d, o), None)
-    sources = (theirs, 0, 2, 8, 10)
+    sources = (theirs, 4, 6, 12, 14, 0, 2, 16, 18)
+    sources_lists = (2 + o, 0, 1, 4, 5)
     send(speed.at[b], speed.at[b], 2, 2, (d, o), None)
     states = (started[0][0], started.pop()[0])
     del started[0]
+    for j in range(5):
+        send(
+            lists_sent.at[2 + b],
+            lists_sent.at[homes[j]],
+            12 + j,
+            12 + marks[j],
+            peers[j],
+            there[j],
+        )
 
     arrived(pdx.at[pl.ds(theirs, 2)], 3, None)
     ids[pl.ds(o, 1), :] = pdx[theirs, 5:6, :].astype(I32)
@@ -316,23 +350,54 @@
     OX, OY, REST, INFL0, NX, NY, STR, INFL = range(8)
     cur[...] = vel[...]
 
-    def pair(p):
-        return p // 3, p % 3
+    def keep_pair(into, p, far, me):
+        far_t = pdx[far].T
+        for q in range(0, 128, 32):
+            rows = slice(q, q + 32)
+            ox = far_t[rows, 0:1] - me[0:1, :]
+            oy = far_t[rows, 1:2] - me[1:2, :]
+            r2 = ox * ox + oy * oy
+            into[OX, p, rows] = ox
+            into[OY, p, rows] = oy
+            into[REST, p, rows] = jnp.sqrt(r2 + CORE_SQ)
+            into[INFL0, p, rows] = jnp.exp(-0.5 * r2)
+
+    def named(p):
+        return family[p // 3, p % 3]
+
+    def named_far(f, k):
+        listed = lists[lax.shift_right_arithmetic(f, 1), lax.bitwise_and(f, 1), k]
+        return listed + lax.shift_left(lax.shift_right_arithmetic(f, 2), 2)
 
     def keep_bonds():
         for p in range(6):
-            t, k = pair(p)
-            far_t = pdx[family[t, k]].T
-            me = pdx[own + t]
-            for q in range(0, 128, 32):
-                rows = slice(q, q + 32)
-                ox = far_t[rows, 0:1] - me[0:1, :]
-                oy = far_t[rows, 1:2] - me[1:2, :]
-                r2 = ox * ox + oy * oy
-                bonds[OX, p, rows] = ox
-                bonds[OY, p, rows] = oy
-                bonds[REST, p, rows] = jnp.sqrt(r2 + CORE_SQ)
-                bonds[INFL0, p, rows] = jnp.exp(-0.5 * r2)
+            keep_pair(bonds, p, named(p) + 4, pdx[own + p // 3])
+
+        @pl.loop(0, 6)
+        def _(p):
+            t = p // 3
+            f = family[t, p - 3 * t]
+            me = pdx[f + 4]
+            for k in range(3):
+                keep_pair(far_bonds, 3 * p + k, named_far(f, k), me)
+
+    def stretched(kept, p, rows, ub, far_t, me):
+        yx = kept[OX, p, rows] + (far_t[rows, 0:1] - me[0:1, :])
+        yy = kept[OY, p, rows] + (far_t[rows, 1:2] - me[1:2, :])
+        y2 = yx * yx + yy * yy + CORE_SQ
+        inverse = lax.rsqrt(y2)
+        rest = kept[REST, p, rows]
+        stretch = y2 * inverse - rest
+        ratio = stretch * (1.0 / STRETCH)
+        influence = kept[INFL0, p, rows] * inverted(1.0 + ratio * ratio)
+        return yx, yy, inverse, rest, stretch, influence
+
+    def columns(ub, far):
+        return jnp.concatenate([ub[far], jnp.zeros((6, 128), F32)], axis=0).T
+
+    def state_of(total):
+        dilated, volume = [jnp.sum(x, axis=0, keepdims=True) for x in total]
+        return jnp.concatenate([2.0 * dilated / volume, volume], axis=0)
 
     row_iota = lax.broadcasted_iota(I32, (64, 128), 0)
 
@@ -360,8 +425,8 @@
         return jnp.concatenate(blocks, axis=0).astype(BF16)
 
     for s in range(2):
-        ub, st = (ub0, ub1)[s], (st0, st1)[s]
-        base = 8 + 13 * s
+        ub = (ub0, ub1)[s]
+        base = 17 + 10 * s
         if s == 0:
             arrived(table.at[o], 0, None)
             arrived(pm.at[o], 1, None)
@@ -381,20 +446,26 @@
             targets.append(nt(picked, pm[q], precision=EXACT)[0:2, :])
         for k in range(4):
             if s == 0:
-                u = pdx[4 + k, 3:5, :]
+                u = pdx[8 + k, 3:5, :]
             else:
-                t = k % 2
-                mine = ub[4 + k]
-                u = mine
+                u = ub[8 + k]
             new = u
             for q in range(2):
                 hit = jnp.full((2, 128), ptile[q], I32) == k
                 new = jnp.where(
                     hit, u + pblend[q : q + 1, :] * (targets[q] - u), new
                 )
-            ub[4 + k] = new
-        send(ub.at[pl.ds(4, 4)], ub.at[pl.ds(8, 4)], base, base + 1, (left, b), has_left)
-        send(ub.at[pl.ds(4, 4)], ub.at[pl.ds(0, 4)], base + 1, base, (right, b), has_right)
+            ub[8 + k] = new
+        mine = ub.at[pl.ds(8, 4)]
+        for j, (to, at, peer, cond) in enumerate(
+            (
+                (16, 3, left2, has_left2),
+                (0, 2, right2, has_right2),
+                (12, 1, left, has_left),
+                (4, 0, right, has_right),
+            )
+        ):
+            send(mine, ub.at[pl.ds(to, 4)], base + j, base + at, (peer, b), cond)
 
         @pl.loop(0, 64 // CHUNK)
         def _(i):
@@ -423,52 +494,6 @@
                     ] = jnp.where(
                         few_t[:, q : q + 1] == few_f[2 + side : 3 + side, :], 1.0, 0.0
                     ).astype(BF16)
-
-        if s == 0:
-            for j in range(1, 5):
-                arrived(pdx.at[pl.ds(sources[j], 2)], 3 + j, there[j])
-            keep_bonds()
-
-        arrived(ub.at[pl.ds(0, 4)], base, has_left)
-        arrived(ub.at[pl.ds(8, 4)], base + 1, has_right)
-
-        totals = [[jnp.zeros((8, 128), F32)] * 2 for _ in range(2)]
-        for p in range(6):
-            t, k = pair(p)
-            far_t = jnp.concatenate([ub[family[t, k]], jnp.zeros((6, 128), F32)], axis=0).T
-            me = ub[own + t]
-            for q in range(0, 128, 32):
-                rows = slice(q, q + 32)
-                yx = bonds[OX, p, rows] + (far_t[rows, 0:1] - me[0:1, :])
-                yy = bonds[OY, p, rows] + (far_t[rows, 1:2] - me[1:2, :])
-                y2 = yx * yx + yy * yy + CORE_SQ
-                inverse = lax.rsqrt(y2)
-                length = y2 * inverse
-                rest = bonds[REST, p, rows]
-                stretch = length - rest
-                ratio = stretch * (1.0 / STRETCH)
-                influence = bonds[INFL0, p, rows] * inverted(1.0 + ratio * ratio)
-                bonds[NX, p, rows] = yx * inverse
-                bonds[NY, p, rows] = yy * inverse
-                bonds[STR, p, rows] = stretch
-                bonds[INFL, p, rows] = influence
-                weighted = influence * rest
-                totals[t][0] = totals[t][0] + folded(weighted * stretch)
-                totals[t][1] = totals[t][1] + folded(weighted * rest)
-        totals = [[jnp.sum(x, axis=0, keepdims=True) for x in y] for y in totals]
-
-        for t in range(2):
-            dilated, volume = totals[t]
-            st[own + t] = jnp.concatenate([2.0 * dilated / volume, volume], axis=0)
-        for j in range(5):
-            send(
-                st.at[pl.ds(own, 2)],
-                st.at[pl.ds(slots[j], 2)],
-                base + 2 + j,
-                base + 2 + marks[j],
-                peers[j],
-                there[j],
-            )
 
         grad = jnp.dot(sgrad[...], del_[...], precision=EXACT, preferred_element_type=F32)
         exx = grad[0:64, 0:128]
@@ -515,14 +540,14 @@
         partial = acc[0:128, :] + acc[128:256, :]
         pel_send[s] = partial
         if s == 0:
-            send(pel_send.at[s], pel_recv.at[s], base + 7, base + 7, (d, o), None)
+            send(pel_send.at[s], pel_recv.at[s], base + 4, base + 4, (d, o), None)
         else:
             cut = pl.ds(o * 64, 64)
             send(
                 pel_send.at[s, cut],
                 pel_recv.at[s, cut],
-                base + 7,
-                base + 7,
+                base + 4,
+                base + 4,
                 (d, o),
                 None,
             )
@@ -540,19 +565,68 @@
             )
             border.append(jnp.concatenate(found, axis=0))
 
-        for j in range(5):
-            arrived(st.at[pl.ds(sources[j], 2)], base + 2 + j, there[j])
+        if s == 0:
+            for j in range(1, 9):
+                arrived(pdx.at[pl.ds(sources[j], 2)], 3 + j, there[j])
+            for j in range(5):
+                arrived(lists_sent.at[sources_lists[j]], 12 + j, there[j])
+            scalars = pltpu.make_async_copy(lists_sent, lists, lsem.at[21])
+            scalars.start()
+            scalars.wait()
+            keep_bonds()
+
+        for at, (frm, cond) in enumerate(
+            ((4, has_left), (12, has_right), (0, has_left2), (16, has_right2))
+        ):
+            arrived(ub.at[pl.ds(frm, 4)], base + at, cond)
+
+        @pl.loop(0, 3)
+        def _(i):
+            for j in range(2):
+                p = 2 * i + j
+                t = p // 3
+                f = family[t, p - 3 * t]
+                me = ub[f + 4]
+                total = [jnp.zeros((8, 128), F32)] * 2
+                for k in range(3):
+                    far_t = columns(ub, named_far(f, k))
+                    for q in range(0, 128, 32):
+                        *_, rest, stretch, influence = stretched(
+                            far_bonds, 3 * p + k, slice(q, q + 32), ub, far_t, me
+                        )
+                        weighted = influence * rest
+                        total[0] = total[0] + folded(weighted * stretch)
+                        total[1] = total[1] + folded(weighted * rest)
+                far_state[p] = state_of(total)
+
+        totals = [[jnp.zeros((8, 128), F32)] * 2 for _ in range(2)]
+        for p in range(6):
+            t = p // 3
+            far_t = columns(ub, named(p) + 4)
+            me = ub[own + t]
+            for q in range(0, 128, 32):
+                rows = slice(q, q + 32)
+                yx, yy, inverse, rest, stretch, influence = stretched(
+                    bonds, p, rows, ub, far_t, me
+                )
+                bonds[NX, p, rows] = yx * inverse
+                bonds[NY, p, rows] = yy * inverse
+                bonds[STR, p, rows] = stretch
+                bonds[INFL, p, rows] = influence
+                weighted = influence * rest
+                totals[t][0] = totals[t][0] + folded(weighted * stretch)
+                totals[t][1] = totals[t][1] + folded(weighted * rest)
+        states_own = [state_of(x) for x in totals]
 
         def coefficients(k, state):
             theta, volume = state[0:1, :], state[1:2, :]
             return 2.0 * k * theta / volume, 4.0 * k / volume, 0.5 * theta
 
         totals = [[jnp.zeros((8, 128), F32)] * 2 for _ in range(2)]
-        near = [coefficients(pdx[own + t][2:3, :], st[own + t]) for t in range(2)]
+        near = [coefficients(pdx[own + t][2:3, :], states_own[t]) for t in range(2)]
         for p in range(6):
-            t, k = pair(p)
-            j = family[t, k]
-            far = coefficients(pdx[j][2:3, :], st[j])
+            t = p // 3
+            far = coefficients(pdx[named(p) + 4][2:3, :], far_state[p])
             far_t = jnp.concatenate(far + (jnp.zeros((5, 128), F32),), axis=0).T
             oa, ob, oc = near[t]
             for q in range(0, 128, 32):
@@ -590,7 +664,7 @@
             )
         late = jnp.concatenate(reaction + moved, axis=0)
         late_send[s] = late
-        send(late_send.at[s], late_recv.at[s], base + 8, base + 8, (d, o), None)
+        send(late_send.at[s], late_recv.at[s], base + 5, base + 5, (d, o), None)
         wide = jnp.concatenate(reaction, axis=1)
         top, low = split2(wide)
         met = jnp.dot(
@@ -606,8 +680,8 @@
             send(
                 bd_send.at[s, side],
                 bd_recv.at[s, 2 * (1 - side) + b],
-                base + 9 + j,
-                base + 9 + 2 * (1 - side) + b,
+                base + 6 + j,
+                base + 6 + 2 * (1 - side) + b,
                 peers[1 + j],
                 there[1 + j],
             )
@@ -619,13 +693,28 @@
                 disp_out[t] = moved[t]
                 vel_out[t] = cur[t]
 
-        arrived(late_recv.at[s], base + 8, None)
+        halves = range(2) if s == 0 else (b,)
+        if s == 0:
+            arrived(speed.at[o], 2, None)
+            arrived(pel_recv.at[s], base + 4, None)
+            for copy in states:
+                copy.wait_send()
+        else:
+            arrived(pel_recv.at[s, pl.ds(b * 64, 64)], base + 4, None)
+        for h in halves:
+            for c in range(2):
+                cut = pl.ds(h * 64 + c * 32, 32)
+                rows = slice(c * 32, c * 32 + 32)
+                speed[h, rows, :] = speed[h, rows, :] - speed[h, 64:96, :] * (
+                    pel_send[s, cut, :] + pel_recv[s, cut, :]
+                )
+        arrived(late_recv.at[s], base + 5, None)
         other = late_recv[s]
         if s == 0:
             for t in range(2):
                 ub1[theirs + t] = other[4 + 2 * t : 6 + 2 * t, :]
         for j in range(4):
-            arrived(bd_recv.at[s, j], base + 9 + j, there[1 + j])
+            arrived(bd_recv.at[s, j], base + 6 + j, there[1 + j])
         shared = [
             jnp.where(
                 jnp.full((2, 128), d, I32) > 0, bd_recv[s, 0] + bd_recv[s, 1], 0.0
@@ -650,19 +739,11 @@
             )
         extra = nt(jnp.concatenate(sides, axis=1), onehot[:, 8192:8704])
         acc[0:128, :] = extra[0:128, :] + extra[128:256, :]
-        if s == 0:
-            arrived(speed.at[o], 2, None)
-            arrived(pel_recv.at[s], base + 7, None)
-            for copy in states:
-                copy.wait_send()
-        else:
-            arrived(pel_recv.at[s, pl.ds(b * 64, 64)], base + 7, None)
-        for h in range(2) if s == 0 else (b,):
+        for h in halves:
             for c in range(2):
                 cut = pl.ds(h * 64 + c * 32, 32)
                 rows = slice(c * 32, c * 32 + 32)
-                nodal = acc[cut, :] - (pel_send[s, cut, :] + pel_recv[s, cut, :])
-                v = speed[h, rows, :] + speed[h, 64:96, :] * nodal
+                v = speed[h, rows, :] + speed[h, 64:96, :] * acc[cut, :]
                 speed[h, rows, :] = v
                 table[h, rows, :] = table[h, rows, :] + TIME_STEP * v
 
@@ -748,11 +829,12 @@
             f32(1, 64),
             pltpu.VMEM((1, 113), I32),
             pltpu.VMEM((1, 113), I32),
-            f32(12, 8, 128),
-            f32(12, 2, 128),
-            f32(12, 2, 128),
-            f32(12, 2, 128),
-            f32(12, 2, 128),
+            f32(20, 8, 128),
+            f32(20, 2, 128),
+            f32(20, 2, 128),
+            pltpu.VMEM((2, 3), I32),
+            pltpu.VMEM((6, 8, 128), I32),
+            pltpu.SMEM((6, 8, 128), I32),
             f32(2, 128, 128),
             f32(2, 64, LO),
             f32(2, 96, LO),
@@ -766,6 +848,8 @@
             f32(64, 128),
             f32(256, LO),
             f32(8, 6, 128, 128),
+            f32(4, 18, 128, 128),
+            f32(6, 2, 128),
             f32(2, 2, 128),
             f32(2, 128, LO),
             f32(2, 128, LO),
@@ -775,7 +859,7 @@
             f32(2, 4, 2, 128),
             pltpu.SemaphoreType.DMA((N_COPIES,)),
             pltpu.SemaphoreType.DMA((N_COPIES,)),
-            pltpu.SemaphoreType.DMA((20,)),
+            pltpu.SemaphoreType.DMA((22,)),
         ],
         compiler_params=pltpu.CompilerParams(
             collective_id=0, has_side_effects=True, vmem_limit_bytes=VMEM_BYTES

time: 46.5 us -> 44.9 us (0.966)
  Pallas kernels: 45.1 us -> 43.5 us
    pallas_call x1, Pallas kernels: 44.4 us -> 42.8 us  [shards(): pl.pallas_call(functools.partial(kernel, n_dom), out_shape=[pltpu.VMEM(pd...]
where the time goes in v4:
time: 44.9 us; the launch traced here: 44.7 us
  Pallas kernels  43.5 us (97%)
  between operations  1.29 us (3%)
    pallas_call x1, Pallas kernels, shards(): pl.pallas_call(functools.partial(kernel, n_dom), out_shape=[pltpu.VMEM(pd...  42.8 us

profile of v4, /device:TPU:257, one launch (start us, length us, event | category | flops | bytes accessed | tf_op | source)
XLA Modules:
  0.0 44.7 jit_solution(3660328572712111470)
XLA Ops:
  1.3 42.8 %shard_map.219 = (f32[2,2,128]{2,1,0:T(2,128)S(1)}, f32[2,2,128]{2,1,0:T(2,128)S(1)}, f32[2,6400]{1,0:T(2,128)S(1)}, f32[2,6400]{1,0:T(2,128)S(1)}) custom-call(f32[2,2,128]{2,1,0:T(2,128)} %disp_in.1, f32[2,2,128]{2,1,0:T(2,128)} %vel_in.1, f32[2,2,128]{2,1,0:T(2,128)} %coord_in.1, f32[2,128]{1,0:T(2,128)} %modulus_in.1, f32[2,128]{1,0:T(2,128)} %step_in.1, ...), custom_call_target="tpu_custom_call" | custom-call | tf_op jit(solution)/shard_map/pallas_call | solution.py:802
  44.1 0.7 %shard_map.220 = (f32[2,2,128]{2,1,0:T(2,128)}, f32[2,2,128]{2,1,0:T(2,128)}, f32[2,6400]{1,0:T(2,128)}, f32[2,6400]{1,0:T(2,128)}) custom-call(f32[2,2,128]{2,1,0:T(2,128)S(1)} %get-tuple-element.8.refs_0_, f32[2,2,128]{2,1,0:T(2,128)S(1)} %get-tuple-element.9.refs_1_, f32[2,6400]{1,0:T(2,128)S(1)} %get-tuple-element.10.refs_2_, ...), custom_call_target="tpu_custom_call" | custom-call | tf_op jit(solution)/shard_map/pallas_call | solution.py:889

commit v5 on v4

--- a/solution.py
+++ b/solution.py
@@ -93,6 +93,7 @@
     pdx,
     ub0,
     ub1,
+    place,
     lists_in,
     lists_sent,
     lists,
@@ -265,7 +266,7 @@
             lo_iota == jnp.broadcast_to(lo_row, (LO, 128)), 1.0, 0.0
         ).astype(BF16)
 
-    @pl.loop(0, 64 // CHUNK)
+    @pl.loop(0, 64 // CHUNK, unroll=2)
     def _(i):
         node = enodes[pl.ds(pl.multiple_of(i * CHUNK, CHUNK), CHUNK), :]
         hrow[pl.ds(pl.multiple_of(i * CHUNK, CHUNK), CHUNK), :] = table_row(node)
@@ -347,7 +348,7 @@
     for g in range(2):
         onehot[:, 8192 + g * 128 : 8320 + g * 128] = onehot_of(few_lo[g : g + 1, :])
 
-    OX, OY, REST, INFL0, NX, NY, STR, INFL = range(8)
+    REST, INFL0, NX, NY, STR, INFL = range(6)
     cur[...] = vel[...]
 
     def keep_pair(into, p, far, me):
@@ -357,8 +358,6 @@
             ox = far_t[rows, 0:1] - me[0:1, :]
             oy = far_t[rows, 1:2] - me[1:2, :]
             r2 = ox * ox + oy * oy
-            into[OX, p, rows] = ox
-            into[OY, p, rows] = oy
             into[REST, p, rows] = jnp.sqrt(r2 + CORE_SQ)
             into[INFL0, p, rows] = jnp.exp(-0.5 * r2)
 
@@ -373,7 +372,7 @@
         for p in range(6):
             keep_pair(bonds, p, named(p) + 4, pdx[own + p // 3])
 
-        @pl.loop(0, 6)
+        @pl.loop(0, 6, unroll=2)
         def _(p):
             t = p // 3
             f = family[t, p - 3 * t]
@@ -381,9 +380,9 @@
             for k in range(3):
                 keep_pair(far_bonds, 3 * p + k, named_far(f, k), me)
 
-    def stretched(kept, p, rows, ub, far_t, me):
-        yx = kept[OX, p, rows] + (far_t[rows, 0:1] - me[0:1, :])
-        yy = kept[OY, p, rows] + (far_t[rows, 1:2] - me[1:2, :])
+    def stretched(kept, p, rows, far_t, me):
+        yx = far_t[rows, 0:1] - me[0:1, :]
+        yy = far_t[rows, 1:2] - me[1:2, :]
         y2 = yx * yx + yy * yy + CORE_SQ
         inverse = lax.rsqrt(y2)
         rest = kept[REST, p, rows]
@@ -392,8 +391,8 @@
         influence = kept[INFL0, p, rows] * inverted(1.0 + ratio * ratio)
         return yx, yy, inverse, rest, stretch, influence
 
-    def columns(ub, far):
-        return jnp.concatenate([ub[far], jnp.zeros((6, 128), F32)], axis=0).T
+    def columns(far):
+        return jnp.concatenate([place[far], jnp.zeros((6, 128), F32)], axis=0).T
 
     def state_of(total):
         dilated, volume = [jnp.sum(x, axis=0, keepdims=True) for x in total]
@@ -467,7 +466,7 @@
         ):
             send(mine, ub.at[pl.ds(to, 4)], base + j, base + at, (peer, b), cond)
 
-        @pl.loop(0, 64 // CHUNK)
+        @pl.loop(0, 64 // CHUNK, unroll=2)
         def _(i):
             rows = pl.ds(pl.multiple_of(i * CHUNK, CHUNK), CHUNK)
             lanes = pl.ds(pl.multiple_of(i * (CHUNK * 128), CHUNK * 128), CHUNK * 128)
@@ -514,7 +513,7 @@
         fel[...] = jnp.dot(sgt[...], stress, precision=EXACT, preferred_element_type=F32)
         acc[...] = jnp.zeros((256, LO), F32)
 
-        @pl.loop(0, 64 // CHUNK)
+        @pl.loop(0, 64 // CHUNK, unroll=2)
         def _(i):
             rows = pl.ds(pl.multiple_of(i * CHUNK, CHUNK), CHUNK)
             lanes = pl.ds(pl.multiple_of(i * (CHUNK * 128), CHUNK * 128), CHUNK * 128)
@@ -579,6 +578,7 @@
             ((4, has_left), (12, has_right), (0, has_left2), (16, has_right2))
         ):
             arrived(ub.at[pl.ds(frm, 4)], base + at, cond)
+        place[...] = pdx[:, 0:2, :] + ub[...]
 
         @pl.loop(0, 3)
         def _(i):
@@ -586,13 +586,13 @@
                 p = 2 * i + j
                 t = p // 3
                 f = family[t, p - 3 * t]
-                me = ub[f + 4]
+                me = place[f + 4]
                 total = [jnp.zeros((8, 128), F32)] * 2
                 for k in range(3):
-                    far_t = columns(ub, named_far(f, k))
+                    far_t = columns(named_far(f, k))
                     for q in range(0, 128, 32):
                         *_, rest, stretch, influence = stretched(
-                            far_bonds, 3 * p + k, slice(q, q + 32), ub, far_t, me
+                            far_bonds, 3 * p + k, slice(q, q + 32), far_t, me
                         )
                         weighted = influence * rest
                         total[0] = total[0] + folded(weighted * stretch)
@@ -602,12 +602,12 @@
         totals = [[jnp.zeros((8, 128), F32)] * 2 for _ in range(2)]
         for p in range(6):
             t = p // 3
-            far_t = columns(ub, named(p) + 4)
-            me = ub[own + t]
+            far_t = columns(named(p) + 4)
+            me = place[own + t]
             for q in range(0, 128, 32):
                 rows = slice(q, q + 32)
                 yx, yy, inverse, rest, stretch, influence = stretched(
-                    bonds, p, rows, ub, far_t, me
+                    bonds, p, rows, far_t, me
                 )
                 bonds[NX, p, rows] = yx * inverse
                 bonds[NY, p, rows] = yy * inverse
@@ -832,6 +832,7 @@
             f32(20, 8, 128),
             f32(20, 2, 128),
             f32(20, 2, 128),
+            f32(20, 2, 128),
             pltpu.VMEM((2, 3), I32),
             pltpu.VMEM((6, 8, 128), I32),
             pltpu.SMEM((6, 8, 128), I32),
@@ -847,8 +848,8 @@
             f32(64, 256),
             f32(64, 128),
             f32(256, LO),
-            f32(8, 6, 128, 128),
-            f32(4, 18, 128, 128),
+            f32(6, 6, 128, 128),
+            f32(2, 18, 128, 128),
             f32(6, 2, 128),
             f32(2, 2, 128),
             f32(2, 128, LO),

time: 44.9 us -> 41.7 us (0.929)
  Pallas kernels: 43.5 us -> 40.3 us
    pallas_call x1, Pallas kernels: 42.8 us -> 39.6 us  [shards(): pl.pallas_call(functools.partial(kernel, n_dom), out_shape=[pltpu.VMEM(pd...]
where the time goes in v5:
time: 41.7 us; the launch traced here: 41.6 us
  Pallas kernels  40.3 us (97%)
  between operations  1.29 us (3%)
    pallas_call x1, Pallas kernels, shards(): pl.pallas_call(functools.partial(kernel, n_dom), out_shape=[pltpu.VMEM(pd...  39.6 us

profile of v5, /device:TPU:257, one launch (start us, length us, event | category | flops | bytes accessed | tf_op | source)
XLA Modules:
  0.0 41.6 jit_solution(15517366745347808283)
XLA Ops:
  1.3 39.6 %shard_map.219 = (f32[2,2,128]{2,1,0:T(2,128)S(1)}, f32[2,2,128]{2,1,0:T(2,128)S(1)}, f32[2,6400]{1,0:T(2,128)S(1)}, f32[2,6400]{1,0:T(2,128)S(1)}) custom-call(f32[2,2,128]{2,1,0:T(2,128)} %disp_in.1, f32[2,2,128]{2,1,0:T(2,128)} %vel_in.1, f32[2,2,128]{2,1,0:T(2,128)} %coord_in.1, f32[2,128]{1,0:T(2,128)} %modulus_in.1, f32[2,128]{1,0:T(2,128)} %step_in.1, ...), custom_call_target="tpu_custom_call" | custom-call | tf_op jit(solution)/shard_map/pallas_call | solution.py:802
  40.9 0.7 %shard_map.220 = (f32[2,2,128]{2,1,0:T(2,128)}, f32[2,2,128]{2,1,0:T(2,128)}, f32[2,6400]{1,0:T(2,128)}, f32[2,6400]{1,0:T(2,128)}) custom-call(f32[2,2,128]{2,1,0:T(2,128)S(1)} %get-tuple-element.8.refs_0_, f32[2,2,128]{2,1,0:T(2,128)S(1)} %get-tuple-element.9.refs_1_, f32[2,6400]{1,0:T(2,128)S(1)} %get-tuple-element.10.refs_2_, ...), custom_call_target="tpu_custom_call" | custom-call | tf_op jit(solution)/shard_map/pallas_call | solution.py:890

commit v6 on v5

--- a/solution.py
+++ b/solution.py
@@ -37,6 +37,11 @@
 def inverted(x):
     y = pl.reciprocal(x, approx=True)
     return y * (2.0 - x * y)
+
+
+def two_parts(x):
+    top, low = split2(x)
+    return jnp.concatenate([top, low, jnp.zeros((12, x.shape[1]), BF16)], axis=0)
 
 
 def nt(a, b, **kw):
@@ -98,6 +103,7 @@
     lists_sent,
     lists,
     pm,
+    split_pm,
     table,
     speed,
     split_table,
@@ -423,37 +429,19 @@
                     blocks.append(wide[c][half * 32 : half * 32 + 32])
         return jnp.concatenate(blocks, axis=0).astype(BF16)
 
-    for s in range(2):
+    def blend(s, picked):
         ub = (ub0, ub1)[s]
         base = 17 + 10 * s
-        if s == 0:
-            arrived(table.at[o], 0, None)
-            arrived(pm.at[o], 1, None)
-
-        top, low = split2(table[...].reshape(128, LO))
-        split_table[0:128, :] = top
-        split_table[128:256, :] = low
-        product = jnp.dot(
-            split_table[...], onehot[:, 8192:8448], preferred_element_type=F32
-        )
         targets = []
         for q in range(2):
-            picked = masked_rows(
-                product[:, q * 128 : (q + 1) * 128], hrow[64 + q : 65 + q, :]
-            )
-            picked = jnp.concatenate(picked + [jnp.zeros((6, 128), F32)], axis=0)
-            targets.append(nt(picked, pm[q], precision=EXACT)[0:2, :])
+            x = nt(two_parts(picked[q]), split_pm[q])
+            targets.append(x[0:2, 0:128] + x[2:4, 0:128] + x[0:2, 128:256])
         for k in range(4):
-            if s == 0:
-                u = pdx[8 + k, 3:5, :]
-            else:
-                u = ub[8 + k]
+            u = pdx[8 + k, 3:5, :] if s == 0 else ub[8 + k]
             new = u
             for q in range(2):
                 hit = jnp.full((2, 128), ptile[q], I32) == k
-                new = jnp.where(
-                    hit, u + pblend[q : q + 1, :] * (targets[q] - u), new
-                )
+                new = jnp.where(hit, u + pblend[q : q + 1, :] * (targets[q] - u), new)
             ub[8 + k] = new
         mine = ub.at[pl.ds(8, 4)]
         for j, (to, at, peer, cond) in enumerate(
@@ -465,6 +453,37 @@
             )
         ):
             send(mine, ub.at[pl.ds(to, 4)], base + j, base + at, (peer, b), cond)
+
+    for s in range(2):
+        ub = (ub0, ub1)[s]
+        base = 17 + 10 * s
+        if s == 0:
+            arrived(table.at[o], 0, None)
+            arrived(pm.at[o], 1, None)
+            for q in range(2):
+                top, low = split2(pm[q])
+                split_pm[q, 0:128] = top
+                split_pm[q, 128:256] = low
+
+        top, low = split2(table[...].reshape(128, LO))
+        split_table[0:128, :] = top
+        split_table[128:256, :] = low
+        if s == 0:
+            product = jnp.dot(
+                split_table[...], onehot[:, 8192:8448], preferred_element_type=F32
+            )
+            blend(
+                0,
+                [
+                    jnp.concatenate(
+                        masked_rows(
+                            product[:, q * 128 : (q + 1) * 128], hrow[64 + q : 65 + q, :]
+                        ),
+                        axis=0,
+                    )
+                    for q in range(2)
+                ],
+            )
 
         @pl.loop(0, 64 // CHUNK, unroll=2)
         def _(i):
@@ -574,11 +593,32 @@
             scalars.wait()
             keep_bonds()
 
-        for at, (frm, cond) in enumerate(
-            ((4, has_left), (12, has_right), (0, has_left2), (16, has_right2))
-        ):
-            arrived(ub.at[pl.ds(frm, 4)], base + at, cond)
-        place[...] = pdx[:, 0:2, :] + ub[...]
+        arrived(ub.at[pl.ds(4, 4)], base, has_left)
+        arrived(ub.at[pl.ds(12, 4)], base + 1, has_right)
+        place[4:16] = pdx[4:16, 0:2, :] + ub[4:16]
+
+        totals = [[jnp.zeros((8, 128), F32)] * 2 for _ in range(2)]
+        for p in range(6):
+            t = p // 3
+            far_t = columns(named(p) + 4)
+            me = place[own + t]
+            for q in range(0, 128, 32):
+                rows = slice(q, q + 32)
+                yx, yy, inverse, rest, stretch, influence = stretched(
+                    bonds, p, rows, far_t, me
+                )
+                bonds[NX, p, rows] = yx * inverse
+                bonds[NY, p, rows] = yy * inverse
+                bonds[STR, p, rows] = stretch
+                bonds[INFL, p, rows] = influence
+                weighted = influence * rest
+                totals[t][0] = totals[t][0] + folded(weighted * stretch)
+                totals[t][1] = totals[t][1] + folded(weighted * rest)
+        states_own = [state_of(x) for x in totals]
+        arrived(ub.at[pl.ds(0, 4)], base + 2, has_left2)
+        arrived(ub.at[pl.ds(16, 4)], base + 3, has_right2)
+        place[0:4] = pdx[0:4, 0:2, :] + ub[0:4]
+        place[16:20] = pdx[16:20, 0:2, :] + ub[16:20]
 
         @pl.loop(0, 3)
         def _(i):
@@ -599,25 +639,6 @@
                         total[1] = total[1] + folded(weighted * rest)
                 far_state[p] = state_of(total)
 
-        totals = [[jnp.zeros((8, 128), F32)] * 2 for _ in range(2)]
-        for p in range(6):
-            t = p // 3
-            far_t = columns(named(p) + 4)
-            me = place[own + t]
-            for q in range(0, 128, 32):
-                rows = slice(q, q + 32)
-                yx, yy, inverse, rest, stretch, influence = stretched(
-                    bonds, p, rows, far_t, me
-                )
-                bonds[NX, p, rows] = yx * inverse
-                bonds[NY, p, rows] = yy * inverse
-                bonds[STR, p, rows] = stretch
-                bonds[INFL, p, rows] = influence
-                weighted = influence * rest
-                totals[t][0] = totals[t][0] + folded(weighted * stretch)
-                totals[t][1] = totals[t][1] + folded(weighted * rest)
-        states_own = [state_of(x) for x in totals]
-
         def coefficients(k, state):
             theta, volume = state[0:1, :], state[1:2, :]
             return 2.0 * k * theta / volume, 4.0 * k / volume, 0.5 * theta
@@ -658,20 +679,15 @@
             for t in range(2):
                 hit = jnp.full((2, 128), ptile[q], I32) == 2 * b + t
                 w = w + jnp.where(hit, pblend[q : q + 1, :] * forces[t], 0.0)
-            w = jnp.concatenate([w, jnp.zeros((6, 128), F32)], axis=0)
-            reaction.append(
-                jnp.dot(w, pm[q], precision=EXACT, preferred_element_type=F32)[0:2, :]
-            )
+            w = two_parts(w)
+            x = jnp.dot(w, split_pm[q, 0:128], preferred_element_type=F32)
+            y = jnp.dot(w, split_pm[q, 128:256], preferred_element_type=F32)
+            reaction.append(x[0:2, :] + x[2:4, :] + y[0:2, :])
         late = jnp.concatenate(reaction + moved, axis=0)
         late_send[s] = late
         send(late_send.at[s], late_recv.at[s], base + 5, base + 5, (d, o), None)
         wide = jnp.concatenate(reaction, axis=1)
-        top, low = split2(wide)
-        met = jnp.dot(
-            jnp.concatenate([top, low, jnp.zeros((12, 256), BF16)], axis=0),
-            link[...],
-            preferred_element_type=F32,
-        )
+        met = jnp.dot(two_parts(wide), link[...], preferred_element_type=F32)
         met = met[0:2, :] + met[2:4, :]
         for side in range(2):
             bd_send[s, side] = met[:, side * 128 : (side + 1) * 128] - border[side]
@@ -707,6 +723,36 @@
                 rows = slice(c * 32, c * 32 + 32)
                 speed[h, rows, :] = speed[h, rows, :] - speed[h, 64:96, :] * (
                     pel_send[s, cut, :] + pel_recv[s, cut, :]
+                )
+        if s == 0:
+            rows = []
+            for h in range(2):
+                for c in range(2):
+                    cut = slice(c * 32, c * 32 + 32)
+                    rows.append(table[h, cut, :] + TIME_STEP * speed[h, cut, :])
+            rows = rows + [speed[0, 64:96, :], speed[1, 64:96, :]]
+            top, low = split2(jnp.concatenate(rows, axis=0))
+            product = jnp.dot(
+                jnp.concatenate([top, low], axis=0),
+                onehot[:, 8192:8448],
+                preferred_element_type=F32,
+            )
+            early, pace = [], []
+            for q in range(2):
+                row = hrow[64 + q : 65 + q, :]
+                part = product[:, q * 128 : (q + 1) * 128]
+                early.append(
+                    jnp.concatenate(
+                        masked_rows(
+                            jnp.concatenate([part[0:128], part[192:320]], axis=0), row
+                        ),
+                        axis=0,
+                    )
+                )
+                steps = part[128:192] + part[320:384]
+                hit = row_iota == jnp.broadcast_to(row, (64, 128))
+                pace.append(
+                    jnp.sum(jnp.where(hit, steps, 0.0), axis=0, keepdims=True)
                 )
         arrived(late_recv.at[s], base + 5, None)
         other = late_recv[s]
@@ -725,6 +771,23 @@
                 0.0,
             ),
         ]
+        if s == 0:
+            met = nt(two_parts(jnp.concatenate(shared, axis=1)), link[...])
+            met = met[0:2, :] + met[2:4, :]
+            blend(
+                1,
+                [
+                    early[q]
+                    + TIME_STEP
+                    * pace[q]
+                    * (
+                        late[2 * q : 2 * q + 2, :]
+                        + other[2 * q : 2 * q + 2, :]
+                        + met[:, q * 128 : (q + 1) * 128]
+                    )
+                    for q in range(2)
+                ],
+            )
         sides = []
         for g, x in enumerate(
             [late[0:2, :] + other[0:2, :], late[2:4, :] + other[2:4, :]] + shared
@@ -837,6 +900,7 @@
             pltpu.VMEM((6, 8, 128), I32),
             pltpu.SMEM((6, 8, 128), I32),
             f32(2, 128, 128),
+            pltpu.VMEM((2, 256, 128), BF16),
             f32(2, 64, LO),
             f32(2, 96, LO),
             pltpu.VMEM((256, LO), BF16),

time: 41.7 us -> 41.5 us (level)
  no operation moved by 1% of the time
where the time goes in v6:
time: 41.5 us; the launch traced here: 41.4 us
  Pallas kernels  40.1 us (97%)
  between operations  1.29 us (3%)
    pallas_call x1, Pallas kernels, shards(): pl.pallas_call(functools.partial(kernel, n_dom), out_shape=[pltpu.VMEM(pd...  39.4 us

profile of v6, /device:TPU:257, one launch (start us, length us, event | category | flops | bytes accessed | tf_op | source)
XLA Modules:
  0.0 41.4 jit_solution(12281171365395905220)
XLA Ops:
  1.3 39.4 %shard_map.219 = (f32[2,2,128]{2,1,0:T(2,128)S(1)}, f32[2,2,128]{2,1,0:T(2,128)S(1)}, f32[2,6400]{1,0:T(2,128)S(1)}, f32[2,6400]{1,0:T(2,128)S(1)}) custom-call(f32[2,2,128]{2,1,0:T(2,128)} %disp_in.1, f32[2,2,128]{2,1,0:T(2,128)} %vel_in.1, f32[2,2,128]{2,1,0:T(2,128)} %coord_in.1, f32[2,128]{1,0:T(2,128)} %modulus_in.1, f32[2,128]{1,0:T(2,128)} %step_in.1, ...), custom_call_target="tpu_custom_call" | custom-call | tf_op jit(solution)/shard_map/pallas_call | solution.py:865
  40.7 0.7 %shard_map.220 = (f32[2,2,128]{2,1,0:T(2,128)}, f32[2,2,128]{2,1,0:T(2,128)}, f32[2,6400]{1,0:T(2,128)}, f32[2,6400]{1,0:T(2,128)}) custom-call(f32[2,2,128]{2,1,0:T(2,128)S(1)} %get-tuple-element.8.refs_0_, f32[2,2,128]{2,1,0:T(2,128)S(1)} %get-tuple-element.9.refs_1_, f32[2,6400]{1,0:T(2,128)S(1)} %get-tuple-element.10.refs_2_, ...), custom_call_target="tpu_custom_call" | custom-call | tf_op jit(solution)/shard_map/pallas_call | solution.py:954

commit v7 on v6

--- a/solution.py
+++ b/solution.py
@@ -272,7 +272,7 @@
             lo_iota == jnp.broadcast_to(lo_row, (LO, 128)), 1.0, 0.0
         ).astype(BF16)
 
-    @pl.loop(0, 64 // CHUNK, unroll=2)
+    @pl.loop(0, 64 // CHUNK, unroll=4)
     def _(i):
         node = enodes[pl.ds(pl.multiple_of(i * CHUNK, CHUNK), CHUNK), :]
         hrow[pl.ds(pl.multiple_of(i * CHUNK, CHUNK), CHUNK), :] = table_row(node)
@@ -378,7 +378,7 @@
         for p in range(6):
             keep_pair(bonds, p, named(p) + 4, pdx[own + p // 3])
 
-        @pl.loop(0, 6, unroll=2)
+        @pl.loop(0, 6, unroll=6)
         def _(p):
             t = p // 3
             f = family[t, p - 3 * t]
@@ -485,7 +485,7 @@
                 ],
             )
 
-        @pl.loop(0, 64 // CHUNK, unroll=2)
+        @pl.loop(0, 64 // CHUNK, unroll=4)
         def _(i):
             rows = pl.ds(pl.multiple_of(i * CHUNK, CHUNK), CHUNK)
             lanes = pl.ds(pl.multiple_of(i * (CHUNK * 128), CHUNK * 128), CHUNK * 128)
@@ -532,7 +532,7 @@
         fel[...] = jnp.dot(sgt[...], stress, precision=EXACT, preferred_element_type=F32)
         acc[...] = jnp.zeros((256, LO), F32)
 
-        @pl.loop(0, 64 // CHUNK, unroll=2)
+        @pl.loop(0, 64 // CHUNK, unroll=4)
         def _(i):
             rows = pl.ds(pl.multiple_of(i * CHUNK, CHUNK), CHUNK)
             lanes = pl.ds(pl.multiple_of(i * (CHUNK * 128), CHUNK * 128), CHUNK * 128)
@@ -620,7 +620,7 @@
         place[0:4] = pdx[0:4, 0:2, :] + ub[0:4]
         place[16:20] = pdx[16:20, 0:2, :] + ub[16:20]
 
-        @pl.loop(0, 3)
+        @pl.loop(0, 3, unroll=3)
         def _(i):
             for j in range(2):
                 p = 2 * i + j

time: 41.5 us -> 40.7 us (0.981)
  Pallas kernels: 40.1 us -> 39.2 us
    pallas_call x1, Pallas kernels: 39.4 us -> 38.5 us  [shards(): pl.pallas_call(functools.partial(kernel, n_dom), out_shape=[pltpu.VMEM(pd...]
where the time goes in v7:
time: 40.7 us; the launch traced here: 40.5 us
  Pallas kernels  39.2 us (96%)
  between operations  1.29 us (3%)
    pallas_call x1, Pallas kernels, shards(): pl.pallas_call(functools.partial(kernel, n_dom), out_shape=[pltpu.VMEM(pd...  38.5 us

profile of v7, /device:TPU:257, one launch (start us, length us, event | category | flops | bytes accessed | tf_op | source)
XLA Modules:
  0.0 40.5 jit_solution(16305472631115659842)
XLA Ops:
  1.3 38.5 %shard_map.219 = (f32[2,2,128]{2,1,0:T(2,128)S(1)}, f32[2,2,128]{2,1,0:T(2,128)S(1)}, f32[2,6400]{1,0:T(2,128)S(1)}, f32[2,6400]{1,0:T(2,128)S(1)}) custom-call(f32[2,2,128]{2,1,0:T(2,128)} %disp_in.1, f32[2,2,128]{2,1,0:T(2,128)} %vel_in.1, f32[2,2,128]{2,1,0:T(2,128)} %coord_in.1, f32[2,128]{1,0:T(2,128)} %modulus_in.1, f32[2,128]{1,0:T(2,128)} %step_in.1, ...), custom_call_target="tpu_custom_call" | custom-call | tf_op jit(solution)/shard_map/pallas_call | solution.py:865
  39.8 0.7 %shard_map.220 = (f32[2,2,128]{2,1,0:T(2,128)}, f32[2,2,128]{2,1,0:T(2,128)}, f32[2,6400]{1,0:T(2,128)}, f32[2,6400]{1,0:T(2,128)}) custom-call(f32[2,2,128]{2,1,0:T(2,128)S(1)} %get-tuple-element.8.refs_0_, f32[2,2,128]{2,1,0:T(2,128)S(1)} %get-tuple-element.9.refs_1_, f32[2,6400]{1,0:T(2,128)S(1)} %get-tuple-element.10.refs_2_, ...), custom_call_target="tpu_custom_call" | custom-call | tf_op jit(solution)/shard_map/pallas_call | solution.py:954

commit v8 on v7

--- a/solution.py
+++ b/solution.py
@@ -429,6 +429,21 @@
                     blocks.append(wide[c][half * 32 : half * 32 + 32])
         return jnp.concatenate(blocks, axis=0).astype(BF16)
 
+    def scattered(values, first):
+        sides = []
+        for g, x in enumerate(values):
+            x_top = x.astype(BF16).astype(F32)
+            x_low = x - x_top
+            sides.append(
+                spread(
+                    [[y[0:1, :], y[1:2, :]] for y in (x_top, x_low)],
+                    hrow[64 + first + g : 65 + first + g, :],
+                )
+            )
+        at = 8192 + first * 128
+        both = nt(jnp.concatenate(sides, axis=1), onehot[:, at : at + 256])
+        return both[0:128, :] + both[128:256, :]
+
     def blend(s, picked):
         ub = (ub0, ub1)[s]
         base = 17 + 10 * s
@@ -759,6 +774,9 @@
         if s == 0:
             for t in range(2):
                 ub1[theirs + t] = other[4 + 2 * t : 6 + 2 * t, :]
+        acc[0:128, :] = scattered(
+            [late[0:2, :] + other[0:2, :], late[2:4, :] + other[2:4, :]], 0
+        )
         for j in range(4):
             arrived(bd_recv.at[s, j], base + 6 + j, there[1 + j])
         shared = [
@@ -788,20 +806,8 @@
                     for q in range(2)
                 ],
             )
-        sides = []
-        for g, x in enumerate(
-            [late[0:2, :] + other[0:2, :], late[2:4, :] + other[2:4, :]] + shared
-        ):
-            x_top = x.astype(BF16).astype(F32)
-            x_low = x - x_top
-            sides.append(
-                spread(
-                    [[y[0:1, :], y[1:2, :]] for y in (x_top, x_low)],
-                    hrow[64 + g : 65 + g, :],
-                )
-            )
-        extra = nt(jnp.concatenate(sides, axis=1), onehot[:, 8192:8704])
-        acc[0:128, :] = extra[0:128, :] + extra[128:256, :]
+        acc[128:256, :] = scattered(shared, 2)
+        acc[0:128, :] = acc[0:128, :] + acc[128:256, :]
         for h in halves:
             for c in range(2):
                 cut = pl.ds(h * 64 + c * 32, 32)

time: 40.7 us -> 40.6 us (level)
  no operation moved by 1% of the time
where the time goes in v8:
time: 40.6 us; the launch traced here: 40.5 us
  Pallas kernels  39.2 us (97%)
  between operations  1.29 us (3%)
    pallas_call x1, Pallas kernels, shards(): pl.pallas_call(functools.partial(kernel, n_dom), out_shape=[pltpu.VMEM(pd...  38.5 us

profile of v8, /device:TPU:257, one launch (start us, length us, event | category | flops | bytes accessed | tf_op | source)
XLA Modules:
  0.0 40.5 jit_solution(7079742912664341735)
XLA Ops:
  1.3 38.5 %shard_map.219 = (f32[2,2,128]{2,1,0:T(2,128)S(1)}, f32[2,2,128]{2,1,0:T(2,128)S(1)}, f32[2,6400]{1,0:T(2,128)S(1)}, f32[2,6400]{1,0:T(2,128)S(1)}) custom-call(f32[2,2,128]{2,1,0:T(2,128)} %disp_in.1, f32[2,2,128]{2,1,0:T(2,128)} %vel_in.1, f32[2,2,128]{2,1,0:T(2,128)} %coord_in.1, f32[2,128]{1,0:T(2,128)} %modulus_in.1, f32[2,128]{1,0:T(2,128)} %step_in.1, ...), custom_call_target="tpu_custom_call" | custom-call | tf_op jit(solution)/shard_map/pallas_call | solution.py:871
  39.8 0.7 %shard_map.220 = (f32[2,2,128]{2,1,0:T(2,128)}, f32[2,2,128]{2,1,0:T(2,128)}, f32[2,6400]{1,0:T(2,128)}, f32[2,6400]{1,0:T(2,128)}) custom-call(f32[2,2,128]{2,1,0:T(2,128)S(1)} %get-tuple-element.8.refs_0_, f32[2,2,128]{2,1,0:T(2,128)S(1)} %get-tuple-element.9.refs_1_, f32[2,6400]{1,0:T(2,128)S(1)} %get-tuple-element.10.refs_2_, ...), custom_call_target="tpu_custom_call" | custom-call | tf_op jit(solution)/shard_map/pallas_call | solution.py:960
